TPU v7x, 128 devices: a whole 4x4x4 slice. The times are simulated.
128 devices in a mesh: tx: 16 (over x, z), ty: 8 (over y, core).
Axes of the slice: x: 4, y: 4, z: 4, core: 2. Of those that a mesh axis runs over, the one named last changes fastest.
Arguments:
- points: bfloat16 [64, 393216], P(None, ('tx', 'ty')), may hold values from -10 to 10
- right_side: float32 [393216], P(('tx', 'ty')), may hold values from -4 to 6
- near_list: int32 [384, 6], P(('tx', 'ty')), may hold values from -1 to 383, as said below
- leaf_skeleton: int32 [384, 256], P(('tx', 'ty')), may hold values from 0 to 1023, as said below
- top_index: int32 [4096], P(('tx', 'ty')), may hold values from 0 to 767, as said below
Outputs:
- solution_field: float32 [393216], P(('tx', 'ty'))
- residual: float32 [393216], P(('tx', 'ty'))
Inputs may be any that keep to these rules, and one draw needn't show every extreme that they name: `near_list`: each non-empty entry names a leaf of the device with the same ty index whose tx index lies at most 2 away along tx, counted cyclically. The lists are symmetric: m stands in l's list exactly as often as l stands in m's. In every draw the leaves of some device fill all 6 slots. `leaf_skeleton`: each row names 256 different points. `top_index`: each block of 32 entries names different entries.
All inputs are finite; a program needn't handle non-finite values.
Results may differ from a plain program's by a relative error of at most 0.0003.
Values may be sent and summed in bfloat16 or wider, within the bound.
A program may use at most 64 MiB of HBM per device.

v0:
```python
import jax
import jax.numpy as jnp
from jax import lax
from jax.sharding import PartitionSpec as P

REACH = 2
ITERS = 2


width_inv = 1.0 / 20.0
far_weight = 32.0
highest = lax.Precision.HIGHEST


def shifted(block, axis, distance):
    devices = range(lax.axis_size(axis))
    route = [((i - distance) % len(devices), i) for i in devices]
    return lax.ppermute(block, axis, route)


def kernel(targets, sources):
    inner_prod = lax.dot_general(
        targets, sources, (((0,), (0,)), ((), ())), preferred_element_type=jnp.float32
    )
    target_sq = jnp.sum(jnp.square(targets.astype(jnp.float32)), axis=0)
    source_sq = jnp.sum(jnp.square(sources.astype(jnp.float32)), axis=0)
    return jnp.exp((2.0 * inner_prod - target_sq[:, None] - source_sq[None, :]) * width_inv)


def apply_block(targets, sources, vector):
    return jnp.dot(kernel(targets, sources), vector, precision=highest)


def column_block(array, index):
    return lax.dynamic_index_in_dim(array, index, 1, keepdims=False)


def row_block(array, index):
    return lax.dynamic_index_in_dim(array, index, 0, keepdims=False)


def squares(residual):
    return lax.psum(jnp.sum(residual * residual), ("tx", "ty"))


def on_device(points, right_side, near_list, leaf_skeleton, top_index):
    leaves_here = near_list.shape[0]
    slot_count = near_list.shape[1]
    leaf_size = points.shape[1] // leaves_here
    coord_count = points.shape[0]
    skel_size = leaf_skeleton.shape[1]
    tx_count = lax.axis_size("tx")
    ty_count = lax.axis_size("ty")
    my_row = lax.axis_index("tx")
    own_blocks = points.reshape(coord_count, leaves_here, leaf_size)
    leaf_major = jnp.moveaxis(own_blocks, 1, 0)
    skeleton = jax.vmap(
        lambda source, chosen: jnp.take(source, chosen, axis=1), in_axes=(1, 0), out_axes=1
    )(own_blocks, leaf_skeleton)
    skeleton = skeleton.reshape(coord_count, leaves_here * skel_size)
    anterp = [
        kernel(skeleton[:, leaf_no * skel_size : (leaf_no + 1) * skel_size], own_blocks[:, leaf_no])
        for leaf_no in range(leaves_here)
    ]
    mine_top = jnp.take(skeleton, top_index, axis=1)
    all_top = lax.all_gather(mine_top, ("tx", "ty"), axis=1, tiled=True)
    group_size = top_index.shape[0] * ty_count
    group_top = lax.dynamic_slice_in_dim(all_top, my_row * group_size, group_size, 1)
    upward = kernel(group_top, skeleton)
    across = kernel(group_top, all_top)
    scale_leaf = 0.25
    scale_group = leaf_size / (leaves_here * ty_count * skel_size)
    scale_top = leaf_size / (tx_count * group_size)
    named = jnp.maximum(near_list, 0)
    owner_row = named // leaves_here // ty_count
    row_gap = (owner_row - my_row + tx_count) % tx_count
    offset = jnp.where(row_gap > tx_count // 2, row_gap - tx_count, row_gap)
    local_index = named % leaves_here
    live = near_list >= 0
    degree = jnp.sum(live.astype(jnp.float32), axis=1)
    zero_leaf = jnp.zeros((leaf_size,), jnp.float32)
    block_list = []
    for gap in range(-REACH, REACH + 1):
        if gap == 0:
            block_list.append(points)
        else:
            block_list.append(shifted(points, "tx", -gap))
    wide_points = jnp.concatenate(block_list, axis=1)
    wide_blocks = wide_points.reshape(coord_count, (2 * REACH + 1) * leaves_here, leaf_size)
    candidate = (offset + REACH) * leaves_here + local_index

    def far_term(vector):
        values = vector.reshape(leaves_here, leaf_size)
        weights = (
            jnp.concatenate(
                [
                    jnp.dot(anterp[leaf_no], values[leaf_no], precision=highest)
                    for leaf_no in range(leaves_here)
                ]
            )
            * scale_leaf
        )
        partial_sum = jnp.dot(upward, weights, precision=highest) * scale_group
        group_sum = lax.psum(partial_sum, "ty")
        all_sums = lax.all_gather(group_sum, "tx", axis=0, tiled=True)
        middle = jnp.dot(across, all_sums, precision=highest) * scale_top
        lower_part = jnp.dot(middle, upward, precision=highest) * scale_group
        pieces = lower_part.reshape(leaves_here, skel_size)
        return (
            jnp.concatenate(
                [
                    jnp.dot(pieces[leaf_no], anterp[leaf_no], precision=highest)
                    for leaf_no in range(leaves_here)
                ]
            )
            * scale_leaf
        )

    solution_field = jnp.zeros_like(right_side)
    residual = right_side
    direction = right_side
    norm_now = squares(residual)
    for step in range(ITERS):
        value_list = []
        for near_gap in range(-REACH, REACH + 1):
            if near_gap == 0:
                value_list.append(direction)
            else:
                value_list.append(shifted(direction, "tx", -near_gap))
        wide_values = jnp.concatenate(value_list).reshape((2 * REACH + 1) * leaves_here, leaf_size)
        own_values = direction.reshape(leaves_here, leaf_size)

        def leaf_step(unused, entry):
            own_block, own_vector, leaf_degree, cand_row, live_row = entry
            running = leaf_degree * apply_block(own_block, own_block, own_vector)

            def add_slot(running, slot):
                slot_index, live_flag = slot

                def live_term():
                    return apply_block(
                        own_block,
                        column_block(wide_blocks, slot_index),
                        row_block(wide_values, slot_index),
                    )

                def dead_term():
                    return zero_leaf

                return (running + lax.cond(live_flag, live_term, dead_term), None)

            running, unused_out = lax.scan(add_slot, running, (cand_row, live_row))
            return (unused, running)

        unused_carry, results = lax.scan(
            leaf_step, 0, (leaf_major, own_values, degree, candidate, live)
        )
        image = direction + results.reshape(-1) / slot_count + far_weight * far_term(direction)
        alpha = norm_now / lax.psum(jnp.sum(direction * image), ("tx", "ty"))
        solution_field = solution_field + alpha * direction
        residual = residual - alpha * image
        norm_next = squares(residual)
        direction = residual + norm_next / norm_now * direction
        norm_now = norm_next
    return (solution_field, residual)


def solution(mesh):
    placed = (
        P(None, ("tx", "ty")),
        P(("tx", "ty")),
        P(("tx", "ty"), None),
        P(("tx", "ty"), None),
        P(("tx", "ty")),
    )
    return jax.shard_map(
        on_device,
        mesh=mesh,
        in_specs=placed,
        out_specs=(P(("tx", "ty")), P(("tx", "ty"))),
        check_vma=False,
    )
```

profile of v0, /device:TPU:0, one launch (start us, length us, event | category | flops | bytes accessed | tf_op | source)
XLA Modules:
  0.0 768.9 jit_solution(12195332538368925790)
XLA Ops:
  0.6 6.2 collective-permute-start.7
  16.4 4.4 gather_fusion.1
  22.0 37.9 %all_gather.9 = bf16[64,4096]{0,1:T(8,128)(2,1)S(1)} all-gather(bf16[64,32]{0,1:T(8,128)(2,1)S(1)} %select_bitcast_fusion), channel_id=1, replica_groups=mesh['tx'=16,'ty'=8] {'tx','ty'}, dimensions={1}, use_global_device_ids=true | all-gather | bytes 528384 | tf_op jit(solution)/shard_map/all_gather | solution.py:66
  67.6 13.3 %psum.43 = f32[256]{0:T(256)S(1)} all-reduce(f32[256]{0:T(256)S(1)} %broadcast_multiply_fusion.9), channel_id=1, replica_groups=mesh['tx'=16,'ty'=8] {'ty'}, use_global_device_ids=true, to_apply=%region_21.22 | all-reduce | flops 256 | bytes 2048 | tf_op jit(solution)/shard_map/psum | solution.py:104
  80.9 23.0 %all-gather = f32[16,1,256]{2,1,0:T(1,128)S(1)} all-gather(f32[1,1,256]{2,1,0:T(1,128)S(1)} %bitcast.266), channel_id=1, replica_groups=mesh['tx'=16,'ty'=8] {'tx'}, dimensions={0}, use_global_device_ids=true | all-gather | bytes 17408 | tf_op jit(solution)/shard_map/all_gather | solution.py:105
  108.3 3.3 fusion.120
  117.9 5.4 collective-permute-start.2
  123.7 3.4 concatenate.44
  131.3 3.9 collective-permute-done.3
  136.0 109.9 %while.41 = (s32[]{:T(128)}, f32[3,1024]{1,0:T(4,128)}, f32[3]{0:T(128)}, bf16[3,64,1024]{2,1,0:T(8,128)(2,1)S(1)}, f32[3,1024]{1,0:T(4,128)}, /*index=5*/s32[3,...) while((s32[]{:T(128)}, f32[3,1024]{1,0:T(4,128)}, ...), condition=%wide.region_11.12_spmd, body=%wide.region_3.11_spmd.sunk | while | flops 302578688 | bytes 17768952 | solution.py:155
  140.5 5.2 fusion.195
  146.5 19.6 %while.44 = (s32[]{:T(128)}, f32[1024]{0:T(1024)S(1)}, pred[6]{0:T(512)(128)(4,1)}, s32[6]{0:T(128)}, bf16[64,15,1024]{2,0,1:T(8,128)(2,1)S(1)}, /*index=5*/bf16...) while((s32[]{:T(128)}, f32[1024]{0:T(1024)S(1)}, pred[6]{0:T(512)(128)(4,1)}, s32[6]{0:T(128)}, ...), condition=%wide.region_10.10_spmd, body=%wide.region_5.9_spmd.sunk | while | flops 151387136 | bytes 8949970 | solution.py:152
  154.3 7.8 %conditional.5 = (f32[1024]{0:T(1024)S(1)}) conditional(s32[]{:T(128)} %bitcast.206, () %tuple.116, (s32[6]{0:T(128)}, s32[]{:T(128)}, bf16[64,15,1024]{2,0,1:T(8,128)(2,1)S(1)}, bf16[64,1024]{1,0:T(8,128)(2,1)S(1)}, f32[15,1024]{1,0:T(8,128)}) %tuple.117), branch_computations={%region_6.5_spmd, %region_7.8_spmd} | conditional | flops 151386112 | bytes 8937538 | solution.py:150
  158.2 3.9 fusion
  172.0 5.2 fusion.195
  177.9 27.4 %while.44 = (s32[]{:T(128)}, f32[1024]{0:T(1024)S(1)}, pred[6]{0:T(512)(128)(4,1)}, s32[6]{0:T(128)}, bf16[64,15,1024]{2,0,1:T(8,128)(2,1)S(1)}, /*index=5*/bf16...) while((s32[]{:T(128)}, f32[1024]{0:T(1024)S(1)}, pred[6]{0:T(512)(128)(4,1)}, s32[6]{0:T(128)}, ...), condition=%wide.region_10.10_spmd, body=%wide.region_5.9_spmd.sunk | while | flops 151387136 | bytes 8949970 | solution.py:152
  181.8 7.8 %conditional.5 = (f32[1024]{0:T(1024)S(1)}) conditional(s32[]{:T(128)} %bitcast.206, () %tuple.116, (s32[6]{0:T(128)}, s32[]{:T(128)}, bf16[64,15,1024]{2,0,1:T(8,128)(2,1)S(1)}, bf16[64,1024]{1,0:T(8,128)(2,1)S(1)}, f32[15,1024]{1,0:T(8,128)}) %tuple.117), branch_computations={%region_6.5_spmd, %region_7.8_spmd} | conditional | flops 151386112 | bytes 8937538 | solution.py:150
  185.7 3.9 fusion
  191.5 7.8 %conditional.5 = (f32[1024]{0:T(1024)S(1)}) conditional(s32[]{:T(128)} %bitcast.206, () %tuple.116, (s32[6]{0:T(128)}, s32[]{:T(128)}, bf16[64,15,1024]{2,0,1:T(8,128)(2,1)S(1)}, bf16[64,1024]{1,0:T(8,128)(2,1)S(1)}, f32[15,1024]{1,0:T(8,128)}) %tuple.117), branch_computations={%region_6.5_spmd, %region_7.8_spmd} | conditional | flops 151386112 | bytes 8937538 | solution.py:150
  195.5 3.9 fusion
  211.2 5.2 fusion.195
  217.1 27.4 %while.44 = (s32[]{:T(128)}, f32[1024]{0:T(1024)S(1)}, pred[6]{0:T(512)(128)(4,1)}, s32[6]{0:T(128)}, bf16[64,15,1024]{2,0,1:T(8,128)(2,1)S(1)}, /*index=5*/bf16...) while((s32[]{:T(128)}, f32[1024]{0:T(1024)S(1)}, pred[6]{0:T(512)(128)(4,1)}, s32[6]{0:T(128)}, ...), condition=%wide.region_10.10_spmd, body=%wide.region_5.9_spmd.sunk | while | flops 151387136 | bytes 8949970 | solution.py:152
  224.9 7.8 %conditional.5 = (f32[1024]{0:T(1024)S(1)}) conditional(s32[]{:T(128)} %bitcast.206, () %tuple.116, (s32[6]{0:T(128)}, s32[]{:T(128)}, bf16[64,15,1024]{2,0,1:T(8,128)(2,1)S(1)}, bf16[64,1024]{1,0:T(8,128)(2,1)S(1)}, f32[15,1024]{1,0:T(8,128)}) %tuple.117), branch_computations={%region_6.5_spmd, %region_7.8_spmd} | conditional | flops 151386112 | bytes 8937538 | solution.py:150
  228.9 3.9 fusion
  234.7 7.8 %conditional.5 = (f32[1024]{0:T(1024)S(1)}) conditional(s32[]{:T(128)} %bitcast.206, () %tuple.116, (s32[6]{0:T(128)}, s32[]{:T(128)}, bf16[64,15,1024]{2,0,1:T(8,128)(2,1)S(1)}, bf16[64,1024]{1,0:T(8,128)(2,1)S(1)}, f32[15,1024]{1,0:T(8,128)}) %tuple.117), branch_computations={%region_6.5_spmd, %region_7.8_spmd} | conditional | flops 151386112 | bytes 8937538 | solution.py:150
  238.6 3.9 fusion
  247.9 163.8 %all-reduce = (f32[]{:T(128)}, f32[]{:T(128)}) all-reduce(f32[]{:T(128)} %get-tuple-element.273, f32[]{:T(128)} %get-tuple-element.272), channel_id=1, replica_groups=mesh['tx'=16,'ty'=8] {'tx','ty'}, use_global_device_ids=true, to_apply=%region_1.2 | all-reduce | flops 2 | bytes 16 | tf_op jit(solution)/shard_map/psum | solution.py:43
  414.5 62.2 %psum.45 = f32[]{:T(128)} all-reduce(f32[]{:T(128)} %get-tuple-element.344), channel_id=1, replica_groups=mesh['tx'=16,'ty'=8] {'tx','ty'}, use_global_device_ids=true, to_apply=%region_25.26 | all-reduce | flops 1 | bytes 8 | tf_op jit(solution)/shard_map/psum | solution.py:43
  478.7 3.4 collective-permute-start.11
  492.0 12.9 %psum.46 = f32[256]{0:T(256)S(1)} all-reduce(f32[256]{0:T(256)S(1)} %broadcast_multiply_fusion.8), channel_id=1, replica_groups=mesh['tx'=16,'ty'=8] {'ty'}, use_global_device_ids=true, to_apply=%region_35.36 | all-reduce | flops 256 | bytes 2048 | tf_op jit(solution)/shard_map/psum | solution.py:104
  504.9 23.6 %all-gather.1 = f32[16,1,256]{2,1,0:T(1,128)S(1)} all-gather(f32[1,1,256]{2,1,0:T(1,128)S(1)} %bitcast.267), channel_id=1, replica_groups=mesh['tx'=16,'ty'=8] {'tx'}, dimensions={0}, use_global_device_ids=true | all-gather | bytes 17408 | tf_op jit(solution)/shard_map/all_gather | solution.py:105
  528.4 5.5 fusion.128
  536.9 83.1 %while.43 = (s32[]{:T(128)}, f32[3,1024]{1,0:T(4,128)S(1)}, f32[3]{0:T(128)}, bf16[3,64,1024]{2,1,0:T(8,128)(2,1)S(1)}, f32[3,1024]{1,0:T(4,128)S(1)}, /*index=5...) while((s32[]{:T(128)}, f32[3,1024]{1,0:T(4,128)S(1)}, ...), condition=%wide.region_34.35_spmd, body=%wide.region_26.34_spmd.sunk | while | flops 302578688 | bytes 17768952 | solution.py:155
  540.4 4.5 fusion.202
  545.6 14.6 %while.45 = (s32[]{:T(128)}, f32[1024]{0:T(1024)S(1)}, pred[6]{0:T(512)(128)(4,1)S(1)}, s32[6]{0:T(128)S(1)}, bf16[64,15,1024]{2,0,1:T(8,128)(2,1)S(1)}, /*index...) while((s32[]{:T(128)}, f32[1024]{0:T(1024)S(1)}, pred[6]{0:T(512)(128)(4,1)S(1)}, ...), condition=%wide.region_33.33_spmd, body=%wide.region_28.32_spmd.sunk | while | flops 151387136 | bytes 8949970 | solution.py:152
  551.0 6.6 conditional.4
  554.3 3.2 fusion.36
  563.8 4.5 fusion.202
  569.0 21.1 %while.45 = (s32[]{:T(128)}, f32[1024]{0:T(1024)S(1)}, pred[6]{0:T(512)(128)(4,1)S(1)}, s32[6]{0:T(128)S(1)}, bf16[64,15,1024]{2,0,1:T(8,128)(2,1)S(1)}, /*index...) while((s32[]{:T(128)}, f32[1024]{0:T(1024)S(1)}, pred[6]{0:T(512)(128)(4,1)S(1)}, ...), condition=%wide.region_33.33_spmd, body=%wide.region_28.32_spmd.sunk | while | flops 151387136 | bytes 8949970 | solution.py:152
  571.6 6.6 conditional.4
  579.5 6.6 conditional.4
  582.9 3.2 fusion.36
  593.6 4.5 fusion.202
  598.8 21.1 %while.45 = (s32[]{:T(128)}, f32[1024]{0:T(1024)S(1)}, pred[6]{0:T(512)(128)(4,1)S(1)}, s32[6]{0:T(128)S(1)}, bf16[64,15,1024]{2,0,1:T(8,128)(2,1)S(1)}, /*index...) while((s32[]{:T(128)}, f32[1024]{0:T(1024)S(1)}, pred[6]{0:T(512)(128)(4,1)S(1)}, ...), condition=%wide.region_33.33_spmd, body=%wide.region_28.32_spmd.sunk | while | flops 151387136 | bytes 8949970 | solution.py:152
  604.2 6.6 conditional.4
  607.6 3.2 fusion.36
  612.0 6.6 conditional.4
  620.7 145.8 %psum.47 = f32[]{:T(128)} all-reduce(f32[]{:T(128)} %multiply_reduce_fusion.15), channel_id=1, replica_groups=mesh['tx'=16,'ty'=8] {'tx','ty'}, use_global_device_ids=true, to_apply=%region_37.38 | all-reduce | flops 1 | bytes 8 | tf_op jit(solution)/shard_map/psum | solution.py:159
  (327 shorter events, 144.6 us)
Async XLA Ops:
  0.6 114.6 %collective-permute-start.7 = (f32[3072]{0:T(1024)}, f32[3072]{0:T(1024)S(1)}, u32[]{:S(2)}, u32[]{:S(2)}) collective-permute-start(f32[3072]{0:T(1024)} %param.18), channel_id=1, source_target_pairs={{16,0},{24,8},{32,16},{40,24},{48,32},{56,40},{64,48},{72,56},{80,... | collective-permute-start | bytes 36872 | tf_op jit(solution)/shard_map/ppermute | solution.py:18
  6.9 111.1 %collective-permute-start.6 = (f32[3072]{0:T(1024)}, f32[3072]{0:T(1024)S(1)}, u32[]{:S(2)}, u32[]{:S(2)}) collective-permute-start(f32[3072]{0:T(1024)} %param.18), channel_id=1, source_target_pairs={{8,0},{16,8},{24,16},{32,24},{40,32},{48,40},{56,48},{64,56},{72,6... | collective-permute-start | bytes 36872 | tf_op jit(solution)/shard_map/ppermute | solution.py:18
  7.6 115.8 %collective-permute-start.5 = (f32[3072]{0:T(1024)}, f32[3072]{0:T(1024)S(1)}, u32[]{:S(2)}, u32[]{:S(2)}) collective-permute-start(f32[3072]{0:T(1024)} %param.18), channel_id=1, source_target_pairs={{120,0},{0,8},{8,16},{16,24},{24,32},{32,40},{40,48},{48,56},{56,6... | collective-permute-start | bytes 36872 | tf_op jit(solution)/shard_map/ppermute | solution.py:18
  8.9 114.8 %collective-permute-start.4 = (f32[3072]{0:T(1024)}, f32[3072]{0:T(1024)S(1)}, u32[]{:S(2)}, u32[]{:S(2)}) collective-permute-start(f32[3072]{0:T(1024)} %param.18), channel_id=1, source_target_pairs={{112,0},{120,8},{0,16},{8,24},{16,32},{24,40},{32,48},{40,56},{48,... | collective-permute-start | bytes 36872 | tf_op jit(solution)/shard_map/ppermute | solution.py:18
  9.9 117.2 %collective-permute-start = (bf16[64,3072]{1,0:T(8,128)(2,1)}, bf16[64,3072]{1,0:T(8,128)(2,1)}, u32[]{:S(2)}, u32[]{:S(2)}) collective-permute-start(bf16[64,3072]{1,0:T(8,128)(2,1)} %param.17), channel_id=1, source_target_pairs={{112,0},{120,8},{0,16},{8,24},{16,32},{24,40},{32,48},{40,56},{48,... | collective-permute-start | bytes 1179656 | tf_op jit(solution)/shard_map/ppermute | solution.py:18
  15.9 47.5 %copy-start.8 = (bf16[64,3072]{0,1:T(8,128)(2,1)}, bf16[64,3072]{0,1:T(8,128)(2,1)S(1)}, u32[]{:S(2)}) copy-start(bf16[64,3072]{0,1:T(8,128)(2,1)S(1)} %copy.15) | copy-start | bytes 1179652
  60.0 2.1 copy-start.9
  62.4 51.0 %copy-start.1 = (f32[256,1024]{1,0:T(8,128)}, f32[256,1024]{1,0:T(8,128)S(1)}, u32[]{:S(2)}) copy-start(f32[256,1024]{1,0:T(8,128)S(1)} %fusion.83) | copy-start | bytes 3145732
  63.8 1.0 copy-start.3
  66.9 44.7 %copy-start.6 = (f32[256,768]{1,0:T(8,128)}, f32[256,768]{1,0:T(8,128)S(1)}, u32[]{:S(2)}) copy-start(f32[256,768]{1,0:T(8,128)S(1)} %fusion.91) | copy-start | bytes 2359300
  106.4 1.9 copy-start
  106.4 6.4 copy-start.4
  106.4 8.2 %copy-start.13 = (s32[3,6]{1,0:T(4,128)S(1)}, s32[3,6]{1,0:T(4,128)}, u32[]{:S(2)}) copy-start(s32[3,6]{1,0:T(4,128)} %param.19) | copy-start | bytes 220
  106.4 10.1 %copy-start.10 = (f32[3072]{0:T(1024)S(1)}, f32[3072]{0:T(1024)}, u32[]{:S(2)}) copy-start(f32[3072]{0:T(1024)} %param.18) | copy-start | bytes 36868
  115.2 13.8 %collective-permute-start.1 = (bf16[64,3072]{1,0:T(8,128)(2,1)}, bf16[64,3072]{1,0:T(8,128)(2,1)S(1)}, u32[]{:S(2)}, u32[]{:S(2)}) collective-permute-start(bf16[64,3072]{1,0:T(8,128)(2,1)} %param.17), channel_id=1, source_target_pairs={{120,0},{0,8},{8,16},{16,24},{24,32},{32,40},{40,48},{48,56},{56,6... | collective-permute-start | bytes 1179656 | tf_op jit(solution)/shard_map/ppermute | solution.py:18
  116.5 18.7 %copy-start.12 = (f32[3,1024]{1,0:T(4,128)}, f32[3,1024]{1,0:T(4,128)S(1)}, u32[]{:S(2)}) copy-start(f32[3,1024]{1,0:T(4,128)S(1)} %reshape.99) | copy-start | bytes 36868
  117.9 13.3 %collective-permute-start.2 = (bf16[64,3072]{1,0:T(8,128)(2,1)}, bf16[64,3072]{1,0:T(8,128)(2,1)S(1)}, u32[]{:S(2)}, u32[]{:S(2)}) collective-permute-start(bf16[64,3072]{1,0:T(8,128)(2,1)} %param.17), channel_id=1, source_target_pairs={{8,0},{16,8},{24,16},{32,24},{40,32},{48,40},{56,48},{64,56},{72,6... | collective-permute-start | bytes 1179656 | tf_op jit(solution)/shard_map/ppermute | solution.py:18
  123.4 11.8 %collective-permute-start.3 = (bf16[64,3072]{1,0:T(8,128)(2,1)}, bf16[64,3072]{1,0:T(8,128)(2,1)S(1)}, u32[]{:S(2)}, u32[]{:S(2)}) collective-permute-start(bf16[64,3072]{1,0:T(8,128)(2,1)} %param.17), channel_id=1, source_target_pairs={{16,0},{24,8},{32,16},{40,24},{48,32},{56,40},{64,48},{72,56},{80,... | collective-permute-start | bytes 1179656 | tf_op jit(solution)/shard_map/ppermute | solution.py:18
  478.7 57.6 %collective-permute-start.11 = (f32[3072]{0:T(1024)S(1)}, f32[3072]{0:T(1024)S(1)}, u32[]{:S(2)}, u32[]{:S(2)}) collective-permute-start(f32[3072]{0:T(1024)S(1)} %multiply_add_fusion.1), channel_id=1, source_target_pairs={{16,0},{24,8},{32,16},{40,24},{48,32},{56,40},{64,48},{72,56},{80,... | collective-permute-start | bytes 36872 | tf_op jit(solution)/shard_map/ppermute | solution.py:18
  482.1 54.3 %collective-permute-start.10 = (f32[3072]{0:T(1024)S(1)}, f32[3072]{0:T(1024)S(1)}, u32[]{:S(2)}, u32[]{:S(2)}) collective-permute-start(f32[3072]{0:T(1024)S(1)} %multiply_add_fusion.1), channel_id=1, source_target_pairs={{8,0},{16,8},{24,16},{32,24},{40,32},{48,40},{56,48},{64,56},{72,6... | collective-permute-start | bytes 36872 | tf_op jit(solution)/shard_map/ppermute | solution.py:18
  482.7 53.7 %collective-permute-start.9 = (f32[3072]{0:T(1024)S(1)}, f32[3072]{0:T(1024)S(1)}, u32[]{:S(2)}, u32[]{:S(2)}) collective-permute-start(f32[3072]{0:T(1024)S(1)} %multiply_add_fusion.1), channel_id=1, source_target_pairs={{120,0},{0,8},{8,16},{16,24},{24,32},{32,40},{40,48},{48,56},{56,6... | collective-permute-start | bytes 36872 | tf_op jit(solution)/shard_map/ppermute | solution.py:18
  484.3 52.1 %collective-permute-start.8 = (f32[3072]{0:T(1024)S(1)}, f32[3072]{0:T(1024)S(1)}, u32[]{:S(2)}, u32[]{:S(2)}) collective-permute-start(f32[3072]{0:T(1024)S(1)} %multiply_add_fusion.1), channel_id=1, source_target_pairs={{112,0},{120,8},{0,16},{8,24},{16,32},{24,40},{32,48},{40,56},{48,... | collective-permute-start | bytes 36872 | tf_op jit(solution)/shard_map/ppermute | solution.py:18
  504.9 29.1 %copy-start.7 = (f32[256,768]{1,0:T(8,128)S(1)}, f32[256,768]{1,0:T(8,128)}, u32[]{:S(2)}) copy-start(f32[256,768]{1,0:T(8,128)} %copy-done.6) | copy-start | bytes 2359300
  504.9 29.7 %copy-start.2 = (f32[256,1024]{1,0:T(8,128)S(1)}, f32[256,1024]{1,0:T(8,128)}, u32[]{:S(2)}) copy-start(f32[256,1024]{1,0:T(8,128)} %copy-done.1) | copy-start | bytes 3145732
  504.9 30.3 %copy-start.5 = (f32[256,1024]{1,0:T(8,128)S(1)}, f32[256,1024]{1,0:T(8,128)}, u32[]{:S(2)}) copy-start(f32[256,1024]{1,0:T(8,128)} %copy-done.3) | copy-start | bytes 3145732
  536.9 230.9 %copy-start.11 = (f32[3072]{0:T(1024)S(1)}, f32[3072]{0:T(1024)}, u32[]{:S(2)}) copy-start(f32[3072]{0:T(1024)} %param.18) | copy-start | bytes 36868
where the time goes:
time: 774 us; the launch traced here: 769 us
  blocking collectives  483 us (62%)
  matrix products  106 us (14%)
  local copies, waits for them, and re-layouts  86.7 us (11%)
  loops' own time  43.1 us (6%)
  starting transfers between devices  22.3 us (3%)
  other arithmetic  17.2 us (2%)
    psum x2, blocking collectives, squares(): return lax.psum(jnp.sum(residual * residual), ('tx', 'ty'))  226 us
    psum x1, blocking collectives, on_device(): alpha = norm_now / lax.psum(jnp.sum(direction * image), ('tx', 'ty'))  146 us
    dot_general x16, matrix products, apply_block(): return jnp.dot(kernel(targets, sources), vector, precision=highest)  64.4 us
    all_gather x2, blocking collectives, far_term(): all_sums = lax.all_gather(group_sum, 'tx', axis=0, tiled=True)  46.6 us
    dynamic_slice x46, local copies, waits for them, and re-layouts, leaf_step(): running, unused_out = lax.scan(add_slot, running, (cand_row, live_row))  44.6 us
    all_gather x1, blocking collectives, on_device(): all_top = lax.all_gather(mine_top, ('tx', 'ty'), axis=1, tiled=True)  37.9 us
    psum x2, blocking collectives, far_term(): group_sum = lax.psum(partial_sum, 'ty')  26.1 us
    another operation x6, loops' own time, leaf_step(): running, unused_out = lax.scan(add_slot, running, (cand_row, live_row))  23.4 us
  transfers between devices with their start and end apart: 12, of which 3 were waited for; matrix products, arithmetic and copies ran while one was open for 7% of the time, Pallas kernels for 0%

commit v1 on v0

v1 whole, which is shorter than its diff:
```python
import functools
import math

import jax
import jax.numpy as jnp
from jax import lax
from jax.experimental import pallas as pl
from jax.experimental.pallas import tpu as pltpu
from jax.sharding import PartitionSpec as P

F32 = jnp.float32
BF16 = jnp.bfloat16
HI = lax.Precision.HIGHEST

D = 64
LEAF = 1024
HALF = 512
SKEL = 256
LDEV = 3
HALVES = LDEV * 2
SLOTS = 6
TSK = 32
N_TX = 16
N_TY = 8
GSKEL = TSK * N_TY
REACH = 2
GAPS = 2 * REACH + 1
ROWS = 8 * GAPS
MINE = 8 * REACH
QUADS = LDEV * SLOTS * 2
CHUNK = 128

SCALE = 2.0 * math.log2(math.e) / 20.0
A_LEAF = 0.25
E_GROUP = LEAF / (LDEV * N_TY * SKEL)
E_TOP = LEAF / (N_TX * GSKEL)
FAR = 32.0


def split3(x):
    high = x.astype(BF16)
    rest = x - high.astype(F32)
    mid = rest.astype(BF16)
    low = (rest - mid.astype(F32)).astype(BF16)
    return high, mid, low


def aux_rows(coords, first):
    wide = coords.astype(F32)
    norm = (-0.5 * SCALE) * jnp.sum(wide * wide, axis=0, keepdims=True)
    high, mid, low = [t.astype(F32) for t in split3(norm)]
    row = lax.broadcasted_iota(jnp.int32, (16, coords.shape[1]), 0)
    lead = 0 if first else 3
    ones = jnp.where((row >= 3 - lead) & (row < 6 - lead), 1.0, 0.0)
    parts = jnp.where(row == lead, high, jnp.where(row == lead + 1, mid, jnp.where(row == lead + 2, low, ones)))
    return parts


def source_form(coords, aux):
    pad = jnp.zeros((48, coords.shape[1]), BF16)
    return jnp.concatenate([coords, coords, coords, aux, pad], axis=0)


def target_form(coords):
    high, mid, low = split3(coords.astype(F32) * SCALE)
    pad = jnp.zeros((48, coords.shape[1]), F32)
    aux = aux_rows(coords, True)
    stack = jnp.concatenate([high.astype(F32), mid.astype(F32), low.astype(F32), aux, pad], axis=0)
    return stack.T.astype(BF16)


def lane_aux(wide, first):
    norm = (-0.5 * SCALE) * jnp.sum(wide * wide, axis=1, keepdims=True)
    high, mid, low = [t.astype(F32) for t in split3(norm)]
    lane = lax.broadcasted_iota(jnp.int32, wide.shape, 1) - D
    lead = 0 if first else 3
    ones = jnp.where((lane >= 3 - lead) & (lane < 6 - lead), 1.0, 0.0)
    return jnp.where(lane == lead, high, jnp.where(lane == lead + 1, mid, jnp.where(lane == lead + 2, low, ones)))


def row_targets(raw):
    wide = raw.astype(F32)
    high, mid, low = [t.astype(F32) for t in split3(wide * SCALE)]
    left = high + pltpu.roll(mid, D, 1)
    right = low + lane_aux(wide, True)
    return jnp.concatenate([left, right], axis=1).astype(BF16)


def row_sources(raw):
    wide = raw.astype(F32)
    left = wide + pltpu.roll(wide, D, 1)
    right = wide + lane_aux(wide, False)
    return jnp.concatenate([left, right], axis=1).astype(BF16)


def to_row(columns):
    ones = jnp.ones((8, 128), F32)
    return lax.dot_general(
        ones, columns, (((1,), (1,)), ((), ())), precision=HI, preferred_element_type=F32
    )[0:1]


def to_column(row):
    parts = []
    for start in range(0, row.shape[1], 128):
        piece = jnp.broadcast_to(row[:, start : start + 128], (128, 128))
        parts.append(piece.T)
    return jnp.concatenate(parts, axis=0) if len(parts) > 1 else parts[0]


def fold_lanes(tile):
    total = tile[:, 0:128]
    for start in range(128, tile.shape[1], 128):
        total = total + tile[:, start : start + 128]
    return total


def fold_rows(tile):
    return jnp.sum(tile.reshape(tile.shape[0] // 8, 8, tile.shape[1]), axis=0)


def tile_lanes(column, width):
    return jnp.concatenate([column] * (width // 128), axis=1)


def body(
    pts_in, rhs_in, near, skel_in, top_in, x_out, r_out,
    pts, aux, vals, taug, vb, acc, kq, kd, ka, ku, kc, cbuf, moh,
    zsend, zin, skp, gg, gt, psend, pin, usend, uin, wsend, win, s_one, s_ty, s_tx, s_two,
    pt_s, pt_r, va_s, va_r, z_s, z_r, g_s, g_r, p_s, p_r, u_s, u_r, w_s, w_r, a_s, a_r, b_s, b_r,
):
    my_tx = lax.axis_index("tx")
    my_ty = lax.axis_index("ty")

    def tx_at(step):
        return lax.rem(my_tx + (step + N_TX), N_TX)

    def ty_at(step):
        return lax.rem(my_ty + (step + N_TY), N_TY)

    def send(src, dst, s_sem, r_sem, **where):
        copy = pltpu.make_async_remote_copy(
            src_ref=src, dst_ref=dst, send_sem=s_sem, recv_sem=r_sem,
            device_id=where, device_id_type=pl.DeviceIdType.MESH,
        )
        return copy

    barrier = pltpu.get_barrier_semaphore()
    for step in range(1, N_TX):
        pl.semaphore_signal(barrier, inc=1, device_id={"tx": tx_at(step)}, device_id_type=pl.DeviceIdType.MESH)
    for step in range(1, N_TY):
        pl.semaphore_signal(barrier, inc=1, device_id={"ty": ty_at(step)}, device_id_type=pl.DeviceIdType.MESH)
    for half in range(HALVES):
        vals[0, MINE + half] = rhs_in[half]
    for half in range(HALVES, 8):
        vals[0, MINE + half] = jnp.zeros((1, HALF), F32)
        vals[1, MINE + half] = jnp.zeros((1, HALF), F32)
    for half in range(HALVES):
        pts[MINE + half] = pts_in[:, half * HALF : (half + 1) * HALF]
    pl.semaphore_wait(barrier, N_TX - 1 + N_TY - 1)

    remote_gaps = [1, -1, 2, -2]
    copies = []
    for number, gap in enumerate(remote_gaps):
        place = 8 * (gap + REACH)
        copy = send(vals.at[0, pl.ds(MINE, 8)], vals.at[0, pl.ds(place, 8)], va_s.at[0, number], va_r.at[0, number], tx=tx_at(-gap))
        copy.start()
        copies.append(copy)
    point_copies = []
    for number, gap in enumerate(remote_gaps):
        place = 8 * (gap + REACH)
        copy = send(
            pts.at[pl.ds(MINE, HALVES)], pts.at[pl.ds(place, HALVES)], pt_s.at[number], pt_r.at[number], tx=tx_at(-gap)
        )
        copy.start()
        point_copies.append(copy)
    value_copies = {0: copies}

    def slot(leaf, number, half):
        named = near[leaf, number]
        live = named >= 0
        named = jnp.maximum(named, 0)
        place = lax.rem(lax.div(named, LDEV * N_TY) - my_tx + (N_TX + REACH), N_TX)
        other = lax.rem(named, LDEV)
        same = place == REACH
        itself = live & same & (other == leaf)
        use = live & jnp.logical_not(itself) & (place < GAPS)
        back = jnp.where((place < REACH) | (same & (other < leaf)), 1, 0)
        other_half = half + back - 2 * half * back
        index = jnp.where(use, 8 * place + 2 * other + other_half, MINE)
        return index, jnp.where(use, 1.0, 0.0), jnp.where(live, 1.0, 0.0) + jnp.where(itself, 1.0, 0.0)

    def split_quad(quad):
        return lax.div(quad, 2 * SLOTS), lax.rem(lax.div(quad, 2), SLOTS), lax.rem(quad, 2)

    def degree(leaf):
        total = 0.0
        for number in range(SLOTS):
            total = total + slot(leaf, number, 0)[2]
        return total

    sub = lax.broadcasted_iota(jnp.int32, (ROWS, 128), 0)
    lane = lax.broadcasted_iota(jnp.int32, (ROWS, 128), 1)

    def mark(quad, table):
        index, use, unused = slot(*split_quad(quad))
        return jnp.where((lane == quad) & (sub == index), use, table)

    table = lax.fori_loop(0, QUADS, mark, jnp.zeros((ROWS, 128), F32))
    for leaf in range(LDEV):
        table = jnp.where((lane == QUADS + leaf) & (sub == MINE + 2 * leaf + 1), degree(leaf), table)
    moh[...] = table
    cbuf[pl.ds(QUADS, 128 - QUADS)] = jnp.zeros((128 - QUADS, HALF), F32)

    def own_forms(half, carry):
        coords = pts[MINE + half]
        taug[half] = target_form(coords)
        aux[MINE + half] = aux_rows(coords, False).astype(BF16)
        return carry

    skp[pl.ds(D, 128 - D)] = jnp.zeros((128 - D, LDEV * SKEL), BF16)
    for leaf in range(LDEV):
        chosen = skel_in[leaf : leaf + 1]
        picked = jnp.zeros((D, SKEL), F32)
        for half in range(2):
            place = lax.broadcasted_iota(jnp.int32, (HALF, SKEL), 0) + half * HALF
            hot = jnp.where(place == chosen, 1.0, 0.0).astype(BF16)
            picked = picked + jnp.dot(pts[MINE + 2 * leaf + half], hot, preferred_element_type=F32)
        skp[0:D, leaf * SKEL : (leaf + 1) * SKEL] = picked.astype(BF16)
    wide_lane = lax.broadcasted_iota(jnp.int32, (1, LDEV * SKEL), 1)
    hot_rows = [jnp.where(wide_lane == top_in[t], 1.0, 0.0) for t in range(TSK)]
    hot = jnp.concatenate(hot_rows, axis=0).astype(BF16)
    mine_top = lax.dot_general(
        hot, skp[...], (((1,), (1,)), ((), ())), preferred_element_type=F32
    ).astype(BF16)
    gg[my_ty] = mine_top
    gt[my_tx] = mine_top
    group_copies = []
    for step in range(1, N_TY):
        copy = send(gg.at[my_ty], gg.at[my_ty], g_s.at[step], g_r.at[step], ty=ty_at(step))
        copy.start()
        group_copies.append(copy)
    for step in range(1, N_TX):
        copy = send(gt.at[my_tx], gt.at[my_tx], g_s.at[N_TY + step], g_r.at[N_TY + step], tx=tx_at(step))
        copy.start()
        group_copies.append(copy)

    lax.fori_loop(0, HALVES, own_forms, 0)

    def spread(it):
        def step(half, carry):
            vb[half] = to_column(vals[it, MINE + half])
            return carry
        lax.fori_loop(0, HALVES, step, 0)

    def skeleton_form(leaf):
        coords = skp[0:D, leaf * SKEL : (leaf + 1) * SKEL]
        return source_form(coords, aux_rows(coords, False).astype(BF16))

    def up_leaf(it):
        parts = []
        for leaf in range(LDEV):
            if it == 0:
                form = skeleton_form(leaf)
            total = jnp.zeros((8, SKEL), F32)
            for half in range(2):
                row = 2 * leaf + half
                if it == 0:
                    ka[row] = jnp.exp2(jnp.dot(taug[row], form, preferred_element_type=F32))
                total = total + fold_rows(ka[row] * tile_lanes(vb[row], SKEL))
            parts.append(jnp.sum(total, axis=0, keepdims=True))
        return jnp.concatenate(parts, axis=1) * A_LEAF

    narrow = lax.broadcasted_iota(jnp.int32, (1, 128), 1)

    def up_group(it, weights):
        partial = to_row(fold_lanes(ku[...] * weights)) * E_GROUP
        for part in range(N_TY):
            tile = partial[:, 128 * (part // 4) : 128 * (part // 4) + 128]
            shift = (128 - TSK * (part % 4)) % 128
            if shift:
                tile = pltpu.roll(tile, shift, 1)
            psend[it, part] = jnp.where(narrow < TSK, tile, 0.0)
        out = []
        pin[it, my_ty] = psend[it, my_ty]
        for step in range(1, N_TY):
            copy = send(psend.at[it, ty_at(step)], pin.at[it, my_ty], p_s.at[it, step], p_r.at[it, step], ty=ty_at(step))
            copy.start()
            out.append(copy)
        return out

    def over_top(it, waiting):
        for copy in waiting:
            copy.wait()
        usend[it] = jnp.sum(pin[it], axis=0)
        uin[it, my_tx] = usend[it]
        out = []
        for step in range(1, N_TX):
            copy = send(usend.at[it], uin.at[it, my_tx], u_s.at[it, step], u_r.at[it, step], tx=tx_at(step))
            copy.start()
            out.append(copy)
        return out

    def across(it, waiting):
        for copy in waiting:
            copy.wait()
        tiles = []
        for tile in range(4):
            total = uin[it, 4 * tile]
            for k in range(1, 4):
                total = total + pltpu.roll(uin[it, 4 * tile + k], TSK * k, 1)
            tiles.append(total)
        upper = jnp.concatenate(tiles, axis=1)
        wsend[it] = to_row(fold_lanes(kc[...] * upper)) * E_TOP
        win[it, my_ty] = wsend[it]
        out = []
        for step in range(1, N_TY):
            copy = send(wsend.at[it], win.at[it, my_ty], w_s.at[it, step], w_r.at[it, step], ty=ty_at(step))
            copy.start()
            out.append(copy)
        return out

    def down(it, waiting):
        for copy in waiting:
            copy.wait()
        middle = to_column(jnp.sum(win[it], axis=0))
        lower = fold_rows(ku[...] * tile_lanes(middle, LDEV * SKEL))
        lower = jnp.sum(lower, axis=0, keepdims=True) * (E_GROUP * A_LEAF * FAR * SLOTS)
        for leaf in range(LDEV):
            weights = lower[:, leaf * SKEL : (leaf + 1) * SKEL]
            for half in range(2):
                row = 2 * leaf + half
                acc[row] += fold_lanes(ka[row] * weights)

    def quadrant(it, store, index, row, form, values, fresh, both):
        total = jnp.zeros((8, HALF), F32)
        for start in range(0, HALF, CHUNK):
            rows = pl.ds(start, CHUNK)
            if it == 0:
                tile = jnp.exp2(jnp.dot(taug[row, rows], form, preferred_element_type=F32))
                store[index, rows] = tile
            else:
                tile = store[index, rows]
            part = fold_lanes(tile * values)
            if fresh:
                acc[row, rows] = part
            else:
                acc[row, rows] += part
            if both:
                total = total + fold_rows(tile * tile_lanes(vb[row, rows], HALF))
        return jnp.sum(total, axis=0, keepdims=True)

    def form_of(index):
        return source_form(pts[index], aux[index])

    def diagonal(it):
        def step(leaf, carry):
            weight = degree(leaf)
            low, high = 2 * leaf, 2 * leaf + 1
            form_low = form_of(MINE + low) if it == 0 else None
            form_high = form_of(MINE + high) if it == 0 else None
            v_low = vals[it, MINE + low] * weight
            v_high = vals[it, MINE + high] * weight
            quadrant(it, kd, 3 * leaf, low, form_low, v_low, True, False)
            quadrant(it, kd, 3 * leaf + 1, high, form_high, v_high, True, False)
            cbuf[pl.ds(QUADS + leaf, 1)] = quadrant(it, kd, 3 * leaf + 2, low, form_high, v_high, False, True)
            return carry
        lax.fori_loop(0, LDEV, step, 0)

    def slots(it, start, stop):
        def step(quad, carry):
            leaf, number, half = split_quad(quad)
            index, use, unused = slot(leaf, number, half)
            form = form_of(index) if it == 0 else None
            values = vals[it, index] * use
            cbuf[pl.ds(quad, 1)] = quadrant(it, kq, quad, 2 * leaf + half, form, values, False, True)
            return carry
        lax.fori_loop(start, stop, step, 0)

    def send_back(it):
        parts = jnp.dot(moh[...], cbuf[...], precision=HI, preferred_element_type=F32)
        for place in range(GAPS):
            zsend[it, place] = parts[8 * place : 8 * place + 8]
        out = []
        for number, gap in enumerate(remote_gaps):
            copy = send(
                zsend.at[it, gap + REACH], zin.at[it, REACH - gap], z_s.at[it, number], z_r.at[it, number], tx=tx_at(gap)
            )
            copy.start()
            out.append(copy)
        return out

    def finish(it, waiting):
        rows = [to_row(acc[half]) for half in range(HALVES)]
        for copy in waiting:
            copy.wait()
        total = zsend[it, REACH]
        for gap in remote_gaps:
            total = total + zin[it, REACH - gap]
        own = jnp.concatenate(rows + [jnp.zeros((8 - HALVES, HALF), F32)], axis=0)
        return (own + total) * (1.0 / SLOTS)

    def own_rows(it):
        return jnp.concatenate([vals[it, MINE + half] for half in range(8)], axis=0)

    def pack(*sums):
        row = jnp.zeros((1, 128), F32)
        for number, value in enumerate(sums):
            row = jnp.where(narrow == number, value, row)
        return row

    def sum_first(number, row):
        s_one[number] = row
        s_ty[number, my_ty] = row
        out = []
        for step in range(1, N_TY):
            copy = send(s_one.at[number], s_ty.at[number, my_ty], a_s.at[number, step], a_r.at[number, step], ty=ty_at(step))
            copy.start()
            out.append(copy)
        return out

    def sum_second(number, waiting):
        for copy in waiting:
            copy.wait()
        row = jnp.sum(s_ty[number], axis=0)
        s_two[number] = row
        s_tx[number, my_tx] = row
        out = []
        for step in range(1, N_TX):
            copy = send(s_two.at[number], s_tx.at[number, my_tx], b_s.at[number, step], b_r.at[number, step], tx=tx_at(step))
            copy.start()
            out.append(copy)
        return out

    def sum_last(number, waiting, count):
        for copy in waiting:
            copy.wait()
        row = jnp.sum(s_tx[number], axis=0)
        return [jnp.sum(jnp.where(narrow == k, row, 0.0), axis=1, keepdims=True) for k in range(count)]

    def dot(one, two):
        return jnp.sum(jnp.sum(one * two, axis=0, keepdims=True), axis=1, keepdims=True)

    spread(0)
    weights = up_leaf(0)
    for copy in group_copies:
        copy.wait()
    group_targets = row_targets(gg[...].reshape(GSKEL, 128))
    group_sources = row_sources(gt[...].reshape(N_TX * TSK, 128))
    for leaf in range(LDEV):
        ku[:, leaf * SKEL : (leaf + 1) * SKEL] = jnp.exp2(
            jnp.dot(group_targets, skeleton_form(leaf), preferred_element_type=F32)
        )
    kc[...] = jnp.exp2(
        lax.dot_general(group_targets, group_sources, (((1,), (1,)), ((), ())), preferred_element_type=F32)
    )
    flight = up_group(0, weights)
    diagonal(0)
    flight = over_top(0, flight)
    for copy in point_copies:
        copy.wait()
    for place in range(GAPS):
        if place != REACH:
            def remote_aux(half, carry, place=place):
                aux[8 * place + half] = aux_rows(pts[8 * place + half], False).astype(BF16)
                return carry
            lax.fori_loop(0, HALVES, remote_aux, 0)
    for copy in value_copies[0]:
        copy.wait()
    flight = across(0, flight)
    slots(0, 0, QUADS)
    back = send_back(0)
    down(0, flight)
    start = own_rows(0)
    first = start + finish(0, back)
    for half in range(HALVES):
        vals[1, MINE + half] = first[half : half + 1]

    copies = []
    for number, gap in enumerate(remote_gaps):
        place = 8 * (gap + REACH)
        copy = send(vals.at[1, pl.ds(MINE, 8)], vals.at[1, pl.ds(place, 8)], va_s.at[1, number], va_r.at[1, number], tx=tx_at(-gap))
        copy.start()
        copies.append(copy)
    sums = sum_first(0, pack(dot(start, start), dot(start, first)))
    spread(1)
    flight = up_group(1, up_leaf(1))
    diagonal(1)
    flight = over_top(1, flight)
    sums = sum_second(0, sums)
    for copy in copies:
        copy.wait()
    slots(1, 0, QUADS // 2)
    flight = across(1, flight)
    norm, curve = sum_last(0, sums, 2)
    alpha = norm / curve
    left = start - alpha * first
    sums = sum_first(1, pack(dot(left, left)))
    slots(1, QUADS // 2, QUADS)
    sums = sum_second(1, sums)
    back = send_back(1)
    down(1, flight)
    second = first + finish(1, back)
    (norm_next,) = sum_last(1, sums, 1)
    beta = norm_next / norm
    direction = left + beta * start
    image = (1.0 + beta) * first - alpha * second
    sums = sum_first(2, pack(dot(direction, image)))
    sums = sum_second(2, sums)
    (curve,) = sum_last(2, sums, 1)
    step = norm_next / curve
    x_out[...] = (alpha * start + step * direction)[0:HALVES]
    r_out[...] = (left - step * image)[0:HALVES]


def on_device(points, right_side, near_list, leaf_skeleton, top_index):
    vmem = pl.BlockSpec(memory_space=pltpu.VMEM)
    smem = pl.BlockSpec(memory_space=pltpu.SMEM)
    dma = pltpu.SemaphoreType.DMA
    out = jax.ShapeDtypeStruct((HALVES, HALF), F32)
    solution_field, residual = pl.pallas_call(
        body,
        out_shape=(out, out),
        in_specs=[vmem, vmem, smem, vmem, smem],
        out_specs=(vmem, vmem),
        scratch_shapes=[
            pltpu.VMEM((ROWS, D, HALF), BF16),
            pltpu.VMEM((ROWS, 16, HALF), BF16),
            pltpu.VMEM((2, ROWS, 1, HALF), F32),
            pltpu.VMEM((HALVES, HALF, 256), BF16),
            pltpu.VMEM((HALVES, HALF, 128), F32),
            pltpu.VMEM((HALVES, HALF, 128), F32),
            pltpu.VMEM((QUADS, HALF, HALF), F32),
            pltpu.VMEM((3 * LDEV, HALF, HALF), F32),
            pltpu.VMEM((HALVES, HALF, SKEL), F32),
            pltpu.VMEM((GSKEL, LDEV * SKEL), F32),
            pltpu.VMEM((GSKEL, N_TX * TSK), F32),
            pltpu.VMEM((128, HALF), F32),
            pltpu.VMEM((ROWS, 128), F32),
            pltpu.VMEM((2, GAPS, 8, HALF), F32),
            pltpu.VMEM((2, GAPS, 8, HALF), F32),
            pltpu.VMEM((128, LDEV * SKEL), BF16),
            pltpu.VMEM((N_TY, TSK, 128), BF16),
            pltpu.VMEM((N_TX, TSK, 128), BF16),
            pltpu.VMEM((2, N_TY, 1, 128), F32),
            pltpu.VMEM((2, N_TY, 1, 128), F32),
            pltpu.VMEM((2, 1, 128), F32),
            pltpu.VMEM((2, N_TX, 1, 128), F32),
            pltpu.VMEM((2, 1, GSKEL), F32),
            pltpu.VMEM((2, N_TY, 1, GSKEL), F32),
            pltpu.VMEM((3, 1, 128), F32),
            pltpu.VMEM((3, N_TY, 1, 128), F32),
            pltpu.VMEM((3, N_TX, 1, 128), F32),
            pltpu.VMEM((3, 1, 128), F32),
            dma((4,)), dma((4,)),
            dma((2, 4)), dma((2, 4)),
            dma((2, 4)), dma((2, 4)),
            dma((N_TX + N_TY,)), dma((N_TX + N_TY,)),
            dma((2, N_TY)), dma((2, N_TY)),
            dma((2, N_TX)), dma((2, N_TX)),
            dma((2, N_TY)), dma((2, N_TY)),
            dma((3, N_TY)), dma((3, N_TY)),
            dma((3, N_TX)), dma((3, N_TX)),
        ],
        compiler_params=pltpu.CompilerParams(
            collective_id=0, has_side_effects=True, vmem_limit_bytes=64 * 1024 * 1024 - 512 * 1024
        ),
        name="ridge_cg",
    )(points, right_side.reshape(HALVES, 1, HALF), near_list, leaf_skeleton, top_index)
    return solution_field.reshape(-1), residual.reshape(-1)


def solution(mesh):
    placed = (
        P(None, ("tx", "ty")),
        P(("tx", "ty")),
        P(("tx", "ty"), None),
        P(("tx", "ty"), None),
        P(("tx", "ty")),
    )
    return jax.shard_map(
        on_device,
        mesh=mesh,
        in_specs=placed,
        out_specs=(P(("tx", "ty")), P(("tx", "ty"))),
        check_vma=False,
    )
```

time: 774 us -> 108 us (0.14)
  blocking collectives: 483 us -> 0 us
  matrix products: 106 us -> 0 us
  Pallas kernels: 0 us -> 106 us
  local copies, waits for them, and re-layouts: 86.7 us -> 1.93 us
  loops' own time: 43.1 us -> 0 us
  starting transfers between devices: 22.3 us -> 0 us
  other arithmetic: 17.2 us -> 0 us
    psum x5 -> x0, blocking collectives: 398 us -> none  [the longest x2 226 us: squares(): return lax.psum(jnp.sum(residual * residual), ('tx', 'ty'))]
    dot_general x55 -> x0, matrix products: 106 us -> none  [the longest x16 64.4 us: apply_block(): return jnp.dot(kernel(targets, sources), vector, precision=highest)]
    pallas_call x0 -> x1, Pallas kernels: none -> 106 us  [on_device(): pl.pallas_call(body, out_shape=(out, out), in_specs=[vmem, vmem, smem, vm...]
    all_gather x3 -> x0, blocking collectives: 84.6 us -> none  [the longest x2 46.6 us: far_term(): all_sums = lax.all_gather(group_sum, 'tx', axis=0, tiled=True)]
    dynamic_slice x52 -> x0, local copies, waits for them, and re-layouts: 52.6 us -> none  [the longest x46 44.6 us: leaf_step(): running, unused_out = lax.scan(add_slot, running, (cand_row, live_row))]
    another operation x44 -> x0, loops' own time: 43.1 us -> none  [the longest x6 23.4 us: leaf_step(): running, unused_out = lax.scan(add_slot, running, (cand_row, live_row))]
    ppermute x12 -> x0, starting transfers between devices: 22.3 us -> none  [shifted(): return lax.ppermute(block, axis, route)]
    squeeze x12 -> x0, local copies, waits for them, and re-layouts: 11.5 us -> none  [on_device(): lax.scan(leaf_step, 0, (leaf_major, own_values, degree, candidate, live))]
  transfers between devices with their start and end apart: 12 -> 0, of which waited for: 3 -> 0; matrix products, arithmetic and copies ran while one was open for 7% -> 0% of each run, Pallas kernels for 0% -> 0%
where the time goes in v1:
time: 108 us
  Pallas kernels  106 us (98%)
  local copies, waits for them, and re-layouts  1.93 us (2%)
    pallas_call x1, Pallas kernels, on_device(): pl.pallas_call(body, out_shape=(out, out), in_specs=[vmem, vmem, smem, vm...  106 us

profile of v1, /device:TPU:0, one launch (start us, length us, event | category | flops | bytes accessed | tf_op | source)
XLA Modules:
  0.0 108.1 jit_solution(2357956254435916757)
XLA Ops:
  0.6 105.5 %ridge_cg.1 = (f32[6,512]{1,0:T(8,128)}, f32[6,512]{1,0:T(8,128)}) custom-call(bf16[64,3072]{1,0:T(8,128)(2,1)} %pts_in.1, f32[6,1,512]{2,1,0:T(1,128)} %bitcast.1, s32[3,6]{1,0:T(4,128)} %near.1, s32[3,256]{1,0:T(4,128)} %skel_in.1, s32[32]{0:T(128)} %top_in.1), custom_call_target="tpu_custom_call" | custom-call | tf_op jit(solution)/shard_map/ridge_cg/pallas_call | solution.py:521
  106.1 0.0 copy-start
  106.2 1.3 %reshape.14 = f32[3072]{0:T(1024)} reshape(f32[6,512]{1,0:T(8,128)} %get-tuple-element.4) | data formatting | bytes 24576 | tf_op jit(solution)/shard_map/reshape | solution.py:570
  107.5 0.0 copy-done
  107.5 0.6 reshape.15
Async XLA Ops:
  106.1 1.3 %copy-start = (f32[6,512]{1,0:T(8,128)S(1)}, f32[6,512]{1,0:T(8,128)}, u32[]{:S(2)}) copy-start(f32[6,512]{1,0:T(8,128)} %get-tuple-element.5) | copy-start | bytes 36868

commit v2 on v1

--- a/solution.py
+++ b/solution.py
@@ -29,6 +29,9 @@
 MINE = 8 * REACH
 QUADS = LDEV * SLOTS * 2
 CHUNK = 128
+WAVES = 2
+PART = HALF // WAVES
+WIDE = SLOTS * PART
 
 SCALE = 2.0 * math.log2(math.e) / 20.0
 A_LEAF = 0.25
@@ -125,12 +128,14 @@
 
 def body(
     pts_in, rhs_in, near, skel_in, top_in, x_out, r_out,
-    pts, aux, vals, taug, vb, acc, kq, kd, ka, ku, kc, cbuf, moh,
+    pts_a, pts_b, aux_a, aux_b, vals, taug, vb, acc, kq, kd, ke, ka, ku, kc, cbuf, moh,
     zsend, zin, skp, gg, gt, psend, pin, usend, uin, wsend, win, s_one, s_ty, s_tx, s_two,
     pt_s, pt_r, va_s, va_r, z_s, z_r, g_s, g_r, p_s, p_r, u_s, u_r, w_s, w_r, a_s, a_r, b_s, b_r,
 ):
     my_tx = lax.axis_index("tx")
     my_ty = lax.axis_index("ty")
+    pts = (pts_a, pts_b)
+    aux = (aux_a, aux_b)
 
     def tx_at(step):
         return lax.rem(my_tx + (step + N_TX), N_TX)
@@ -156,25 +161,57 @@
         vals[0, MINE + half] = jnp.zeros((1, HALF), F32)
         vals[1, MINE + half] = jnp.zeros((1, HALF), F32)
     for half in range(HALVES):
-        pts[MINE + half] = pts_in[:, half * HALF : (half + 1) * HALF]
-    pl.semaphore_wait(barrier, N_TX - 1 + N_TY - 1)
+        for wave in range(WAVES):
+            start = half * HALF + wave * PART
+            pts[wave][MINE + half] = pts_in[:, start : start + PART]
 
     remote_gaps = [1, -1, 2, -2]
-    copies = []
-    for number, gap in enumerate(remote_gaps):
-        place = 8 * (gap + REACH)
-        copy = send(vals.at[0, pl.ds(MINE, 8)], vals.at[0, pl.ds(place, 8)], va_s.at[0, number], va_r.at[0, number], tx=tx_at(-gap))
-        copy.start()
-        copies.append(copy)
-    point_copies = []
-    for number, gap in enumerate(remote_gaps):
-        place = 8 * (gap + REACH)
-        copy = send(
-            pts.at[pl.ds(MINE, HALVES)], pts.at[pl.ds(place, HALVES)], pt_s.at[number], pt_r.at[number], tx=tx_at(-gap)
+
+    def point_copy(wave, leaf, number):
+        gap = remote_gaps[number]
+        source = 8 * (REACH if number < 2 else REACH + gap // 2) + 2 * leaf
+        place = 8 * (gap + REACH) + 2 * leaf
+        return send(
+            pts[wave].at[pl.ds(source, 2)], pts[wave].at[pl.ds(place, 2)],
+            pt_s.at[wave, number, leaf], pt_r.at[wave, number, leaf],
+            tx=tx_at(-1 if gap > 0 else 1),
         )
-        copy.start()
-        point_copies.append(copy)
-    value_copies = {0: copies}
+
+    points_out = {}
+
+    def send_points(wave):
+        for leaf in range(LDEV):
+            for number in range(2):
+                copy = point_copy(wave, leaf, number)
+                copy.start()
+                points_out[wave, leaf, number] = copy
+
+    def pass_on(wave, leaf):
+        for number in range(2):
+            points_out[wave, leaf, number].wait_recv()
+            copy = point_copy(wave, leaf, number + 2)
+            copy.start()
+            points_out[wave, leaf, number + 2] = copy
+
+    def points_here(wave):
+        for leaf in range(LDEV):
+            for number in range(4):
+                copy = points_out[wave, leaf, number]
+                if number >= 2:
+                    copy.wait_recv()
+                copy.wait_send()
+
+    def send_values(it):
+        copies = []
+        for number, gap in enumerate(remote_gaps):
+            place = 8 * (gap + REACH)
+            copy = send(
+                vals.at[it, pl.ds(MINE, 8)], vals.at[it, pl.ds(place, 8)],
+                va_s.at[it, number], va_r.at[it, number], tx=tx_at(-gap),
+            )
+            copy.start()
+            copies.append(copy)
+        return copies
 
     def slot(leaf, number, half):
         named = near[leaf, number]
@@ -212,10 +249,13 @@
     moh[...] = table
     cbuf[pl.ds(QUADS, 128 - QUADS)] = jnp.zeros((128 - QUADS, HALF), F32)
 
+    def own_half(half):
+        return jnp.concatenate([pts[wave][MINE + half] for wave in range(WAVES)], axis=1)
+
     def own_forms(half, carry):
-        coords = pts[MINE + half]
-        taug[half] = target_form(coords)
-        aux[MINE + half] = aux_rows(coords, False).astype(BF16)
+        taug[half] = target_form(own_half(half))
+        for wave in range(WAVES):
+            aux[wave][MINE + half] = aux_rows(pts[wave][MINE + half], False).astype(BF16)
         return carry
 
     skp[pl.ds(D, 128 - D)] = jnp.zeros((128 - D, LDEV * SKEL), BF16)
@@ -225,7 +265,7 @@
         for half in range(2):
             place = lax.broadcasted_iota(jnp.int32, (HALF, SKEL), 0) + half * HALF
             hot = jnp.where(place == chosen, 1.0, 0.0).astype(BF16)
-            picked = picked + jnp.dot(pts[MINE + 2 * leaf + half], hot, preferred_element_type=F32)
+            picked = picked + jnp.dot(own_half(2 * leaf + half), hot, preferred_element_type=F32)
         skp[0:D, leaf * SKEL : (leaf + 1) * SKEL] = picked.astype(BF16)
     wide_lane = lax.broadcasted_iota(jnp.int32, (1, LDEV * SKEL), 1)
     hot_rows = [jnp.where(wide_lane == top_in[t], 1.0, 0.0) for t in range(TSK)]
@@ -235,15 +275,18 @@
     ).astype(BF16)
     gg[my_ty] = mine_top
     gt[my_tx] = mine_top
-    group_copies = []
-    for step in range(1, N_TY):
-        copy = send(gg.at[my_ty], gg.at[my_ty], g_s.at[step], g_r.at[step], ty=ty_at(step))
-        copy.start()
-        group_copies.append(copy)
-    for step in range(1, N_TX):
-        copy = send(gt.at[my_tx], gt.at[my_tx], g_s.at[N_TY + step], g_r.at[N_TY + step], tx=tx_at(step))
-        copy.start()
-        group_copies.append(copy)
+
+    def send_top():
+        near_copies, far_copies = [], []
+        for step in range(1, N_TY):
+            copy = send(gg.at[my_ty], gg.at[my_ty], g_s.at[step], g_r.at[step], ty=ty_at(step))
+            copy.start()
+            near_copies.append(copy)
+        for step in range(1, N_TX):
+            copy = send(gt.at[my_tx], gt.at[my_tx], g_s.at[N_TY + step], g_r.at[N_TY + step], tx=tx_at(step))
+            copy.start()
+            far_copies.append(copy)
+        return near_copies, far_copies
 
     lax.fori_loop(0, HALVES, own_forms, 0)
 
@@ -332,48 +375,59 @@
                 row = 2 * leaf + half
                 acc[row] += fold_lanes(ka[row] * weights)
 
-    def quadrant(it, store, index, row, form, values, fresh, both):
-        total = jnp.zeros((8, HALF), F32)
+    def stretch(it, store, row, form, values, fresh, first):
+        width = values.shape[1]
+        total = jnp.zeros((8, width - first), F32)
         for start in range(0, HALF, CHUNK):
             rows = pl.ds(start, CHUNK)
             if it == 0:
                 tile = jnp.exp2(jnp.dot(taug[row, rows], form, preferred_element_type=F32))
-                store[index, rows] = tile
+                store[rows] = tile
             else:
-                tile = store[index, rows]
+                tile = store[rows]
             part = fold_lanes(tile * values)
             if fresh:
                 acc[row, rows] = part
             else:
                 acc[row, rows] += part
-            if both:
-                total = total + fold_rows(tile * tile_lanes(vb[row, rows], HALF))
-        return jnp.sum(total, axis=0, keepdims=True)
-
-    def form_of(index):
-        return source_form(pts[index], aux[index])
+            if first < width:
+                total = total + fold_rows(tile[:, first:] * tile_lanes(vb[row, rows], width - first))
+        return jnp.sum(total, axis=0, keepdims=True) if first < width else None
+
+    def form_of(wave, index):
+        return source_form(pts[wave][index], aux[wave][index])
 
     def diagonal(it):
         def step(leaf, carry):
             weight = degree(leaf)
             low, high = 2 * leaf, 2 * leaf + 1
-            form_low = form_of(MINE + low) if it == 0 else None
-            form_high = form_of(MINE + high) if it == 0 else None
-            v_low = vals[it, MINE + low] * weight
-            v_high = vals[it, MINE + high] * weight
-            quadrant(it, kd, 3 * leaf, low, form_low, v_low, True, False)
-            quadrant(it, kd, 3 * leaf + 1, high, form_high, v_high, True, False)
-            cbuf[pl.ds(QUADS + leaf, 1)] = quadrant(it, kd, 3 * leaf + 2, low, form_high, v_high, False, True)
+            form = None
+            if it == 0:
+                form = jnp.concatenate(
+                    [form_of(wave, MINE + half) for half in (low, high) for wave in range(WAVES)], axis=1
+                )
+            values = jnp.concatenate([vals[it, MINE + low], vals[it, MINE + high]], axis=1) * weight
+            cbuf[pl.ds(QUADS + leaf, 1)] = stretch(it, kd.at[leaf], low, form, values, True, HALF)
+            if it == 0:
+                form = form[:, HALF:]
+            stretch(it, ke.at[leaf], high, form, values[:, HALF:], True, HALF)
             return carry
         lax.fori_loop(0, LDEV, step, 0)
 
-    def slots(it, start, stop):
-        def step(quad, carry):
-            leaf, number, half = split_quad(quad)
-            index, use, unused = slot(leaf, number, half)
-            form = form_of(index) if it == 0 else None
-            values = vals[it, index] * use
-            cbuf[pl.ds(quad, 1)] = quadrant(it, kq, quad, 2 * leaf + half, form, values, False, True)
+    def slots(it, wave, start, stop):
+        def step(row, carry):
+            leaf, half = lax.div(row, 2), lax.rem(row, 2)
+            forms, values = [], []
+            for number in range(SLOTS):
+                index, use, unused = slot(leaf, number, half)
+                if it == 0:
+                    forms.append(form_of(wave, index))
+                values.append(vals[it, index][:, wave * PART : (wave + 1) * PART] * use)
+            form = jnp.concatenate(forms, axis=1) if it == 0 else None
+            total = stretch(it, kq.at[wave, row], row, form, jnp.concatenate(values, axis=1), False, 0)
+            for number in range(SLOTS):
+                place = 2 * SLOTS * leaf + 2 * number + half
+                cbuf[pl.ds(place, 1), wave * PART : (wave + 1) * PART] = total[:, number * PART : (number + 1) * PART]
             return carry
         lax.fori_loop(start, stop, step, 0)
 
@@ -390,15 +444,24 @@
             out.append(copy)
         return out
 
-    def finish(it, waiting):
+    def near_rows(it):
         rows = [to_row(acc[half]) for half in range(HALVES)]
+        own = jnp.concatenate(rows + [jnp.zeros((8 - HALVES, HALF), F32)], axis=0)
+        given = jnp.zeros((1, 1), F32)
+        for place in range(GAPS):
+            if place != REACH:
+                theirs = jnp.concatenate([vals[it, 8 * place + half] for half in range(8)], axis=0)
+                given = given + dot(zsend[it, place], theirs)
+        return (own + zsend[it, REACH]) * (1.0 / SLOTS), given * (1.0 / SLOTS)
+
+    def near_back(it, waiting):
         for copy in waiting:
             copy.wait()
-        total = zsend[it, REACH]
-        for gap in remote_gaps:
-            total = total + zin[it, REACH - gap]
-        own = jnp.concatenate(rows + [jnp.zeros((8 - HALVES, HALF), F32)], axis=0)
-        return (own + total) * (1.0 / SLOTS)
+        total = zin[it, 0]
+        for place in range(1, GAPS):
+            if place != REACH:
+                total = total + zin[it, place]
+        return total * (1.0 / SLOTS)
 
     def own_rows(it):
         return jnp.concatenate([vals[it, MINE + half] for half in range(8)], axis=0)
@@ -441,66 +504,86 @@
     def dot(one, two):
         return jnp.sum(jnp.sum(one * two, axis=0, keepdims=True), axis=1, keepdims=True)
 
+    lax.fori_loop(0, HALVES, own_forms, 0)
     spread(0)
     weights = up_leaf(0)
-    for copy in group_copies:
+    start = own_rows(0)
+    pl.semaphore_wait(barrier, N_TX - 1 + N_TY - 1)
+
+    group_near, group_far = send_top()
+    values_out = send_values(0)
+    send_points(0)
+    diagonal(0)
+    for copy in group_near:
         copy.wait()
     group_targets = row_targets(gg[...].reshape(GSKEL, 128))
-    group_sources = row_sources(gt[...].reshape(N_TX * TSK, 128))
     for leaf in range(LDEV):
         ku[:, leaf * SKEL : (leaf + 1) * SKEL] = jnp.exp2(
             jnp.dot(group_targets, skeleton_form(leaf), preferred_element_type=F32)
         )
+    flight = up_group(0, weights)
+    for leaf in range(LDEV):
+        pass_on(0, leaf)
+    send_points(1)
+    for copy in group_far:
+        copy.wait()
+    group_sources = row_sources(gt[...].reshape(N_TX * TSK, 128))
     kc[...] = jnp.exp2(
         lax.dot_general(group_targets, group_sources, (((1,), (1,)), ((), ())), preferred_element_type=F32)
     )
-    flight = up_group(0, weights)
-    diagonal(0)
     flight = over_top(0, flight)
-    for copy in point_copies:
+
+    def remote_aux(wave):
+        for place in range(GAPS):
+            if place != REACH:
+                def one(half, carry, place=place):
+                    aux[wave][8 * place + half] = aux_rows(pts[wave][8 * place + half], False).astype(BF16)
+                    return carry
+                lax.fori_loop(0, HALVES, one, 0)
+
+    points_here(0)
+    remote_aux(0)
+    for copy in values_out:
         copy.wait()
-    for place in range(GAPS):
-        if place != REACH:
-            def remote_aux(half, carry, place=place):
-                aux[8 * place + half] = aux_rows(pts[8 * place + half], False).astype(BF16)
-                return carry
-            lax.fori_loop(0, HALVES, remote_aux, 0)
-    for copy in value_copies[0]:
-        copy.wait()
+    slots(0, 0, 0, 2)
+    pass_on(1, 0)
     flight = across(0, flight)
-    slots(0, 0, QUADS)
+    slots(0, 0, 2, 4)
+    pass_on(1, 1)
+    slots(0, 0, 4, 6)
+    pass_on(1, 2)
+    down(0, flight)
+    points_here(1)
+    remote_aux(1)
+    slots(0, 1, 0, HALVES)
     back = send_back(0)
-    down(0, flight)
-    start = own_rows(0)
-    first = start + finish(0, back)
+    partial, given = near_rows(0)
+    local = start + partial
+    sums = sum_first(0, pack(dot(start, start), dot(start, local) + given))
+    first = local + near_back(0, back)
     for half in range(HALVES):
         vals[1, MINE + half] = first[half : half + 1]
 
-    copies = []
-    for number, gap in enumerate(remote_gaps):
-        place = 8 * (gap + REACH)
-        copy = send(vals.at[1, pl.ds(MINE, 8)], vals.at[1, pl.ds(place, 8)], va_s.at[1, number], va_r.at[1, number], tx=tx_at(-gap))
-        copy.start()
-        copies.append(copy)
-    sums = sum_first(0, pack(dot(start, start), dot(start, first)))
+    values_out = send_values(1)
     spread(1)
     flight = up_group(1, up_leaf(1))
+    sums = sum_second(0, sums)
     diagonal(1)
     flight = over_top(1, flight)
-    sums = sum_second(0, sums)
-    for copy in copies:
-        copy.wait()
-    slots(1, 0, QUADS // 2)
-    flight = across(1, flight)
     norm, curve = sum_last(0, sums, 2)
     alpha = norm / curve
     left = start - alpha * first
     sums = sum_first(1, pack(dot(left, left)))
-    slots(1, QUADS // 2, QUADS)
+    for copy in values_out:
+        copy.wait()
+    slots(1, 0, 0, HALVES)
     sums = sum_second(1, sums)
+    flight = across(1, flight)
+    slots(1, 1, 0, HALVES)
     back = send_back(1)
     down(1, flight)
-    second = first + finish(1, back)
+    partial, given = near_rows(1)
+    second = first + partial + near_back(1, back)
     (norm_next,) = sum_last(1, sums, 1)
     beta = norm_next / norm
     direction = left + beta * start
@@ -524,14 +607,17 @@
         in_specs=[vmem, vmem, smem, vmem, smem],
         out_specs=(vmem, vmem),
         scratch_shapes=[
-            pltpu.VMEM((ROWS, D, HALF), BF16),
-            pltpu.VMEM((ROWS, 16, HALF), BF16),
+            pltpu.VMEM((ROWS, D, PART), BF16),
+            pltpu.VMEM((ROWS, D, PART), BF16),
+            pltpu.VMEM((ROWS, 16, PART), BF16),
+            pltpu.VMEM((ROWS, 16, PART), BF16),
             pltpu.VMEM((2, ROWS, 1, HALF), F32),
             pltpu.VMEM((HALVES, HALF, 256), BF16),
             pltpu.VMEM((HALVES, HALF, 128), F32),
             pltpu.VMEM((HALVES, HALF, 128), F32),
-            pltpu.VMEM((QUADS, HALF, HALF), F32),
-            pltpu.VMEM((3 * LDEV, HALF, HALF), F32),
+            pltpu.VMEM((WAVES, HALVES, HALF, WIDE), F32),
+            pltpu.VMEM((LDEV, HALF, LEAF), F32),
+            pltpu.VMEM((LDEV, HALF, HALF), F32),
             pltpu.VMEM((HALVES, HALF, SKEL), F32),
             pltpu.VMEM((GSKEL, LDEV * SKEL), F32),
             pltpu.VMEM((GSKEL, N_TX * TSK), F32),
@@ -552,7 +638,7 @@
             pltpu.VMEM((3, N_TY, 1, 128), F32),
             pltpu.VMEM((3, N_TX, 1, 128), F32),
             pltpu.VMEM((3, 1, 128), F32),
-            dma((4,)), dma((4,)),
+            dma((WAVES, 4, LDEV)), dma((WAVES, 4, LDEV)),
             dma((2, 4)), dma((2, 4)),
             dma((2, 4)), dma((2, 4)),
             dma((N_TX + N_TY,)), dma((N_TX + N_TY,)),

time: 108 us -> 86.6 us (0.80)
  Pallas kernels: 106 us -> 83.8 us
    pallas_call x1, Pallas kernels: 106 us -> 83.8 us  [on_device(): pl.pallas_call(body, out_shape=(out, out), in_specs=[vmem, vmem, smem, vm...]
where the time goes in v2:
time: 86.6 us; the launch traced here: 86.4 us
  Pallas kernels  83.8 us (97%)
  local copies, waits for them, and re-layouts  1.93 us (2%)
    pallas_call x1, Pallas kernels, on_device(): pl.pallas_call(body, out_shape=(out, out), in_specs=[vmem, vmem, smem, vm...  83.8 us
    reshape x2, local copies, waits for them, and re-layouts, on_device(): return (solution_field.reshape(-1), residual.reshape(-1))  1.93 us

profile of v2, /device:TPU:0, one launch (start us, length us, event | category | flops | bytes accessed | tf_op | source)
XLA Modules:
  0.0 86.4 jit_solution(5358745262837949747)
XLA Ops:
  0.6 83.8 %ridge_cg.1 = (f32[6,512]{1,0:T(8,128)}, f32[6,512]{1,0:T(8,128)}) custom-call(bf16[64,3072]{1,0:T(8,128)(2,1)} %pts_in.1, f32[6,1,512]{2,1,0:T(1,128)} %bitcast.1, s32[3,6]{1,0:T(4,128)} %near.1, s32[3,256]{1,0:T(4,128)} %skel_in.1, s32[32]{0:T(128)} %top_in.1), custom_call_target="tpu_custom_call" | custom-call | tf_op jit(solution)/shard_map/ridge_cg/pallas_call | solution.py:604
  84.5 0.0 copy-start
  84.5 1.3 %reshape.14 = f32[3072]{0:T(1024)} reshape(f32[6,512]{1,0:T(8,128)} %get-tuple-element.4) | data formatting | bytes 24576 | tf_op jit(solution)/shard_map/reshape | solution.py:656
  85.8 0.0 copy-done
  85.8 0.6 reshape.15
Async XLA Ops:
  84.5 1.3 %copy-start = (f32[6,512]{1,0:T(8,128)S(1)}, f32[6,512]{1,0:T(8,128)}, u32[]{:S(2)}) copy-start(f32[6,512]{1,0:T(8,128)} %get-tuple-element.5) | copy-start | bytes 36868

commit v3 on v2

--- a/solution.py
+++ b/solution.py
@@ -27,11 +27,11 @@
 GAPS = 2 * REACH + 1
 ROWS = 8 * GAPS
 MINE = 8 * REACH
-QUADS = LDEV * SLOTS * 2
+QUADS = 8 * HALVES
 CHUNK = 128
-WAVES = 2
-PART = HALF // WAVES
-WIDE = SLOTS * PART
+PARTS = (256, 128, 128)
+STARTS = (0, 256, 384)
+WAVES = len(PARTS)
 
 SCALE = 2.0 * math.log2(math.e) / 20.0
 A_LEAF = 0.25
@@ -127,15 +127,17 @@
 
 
 def body(
-    pts_in, rhs_in, near, skel_in, top_in, x_out, r_out,
-    pts_a, pts_b, aux_a, aux_b, vals, taug, vb, acc, kq, kd, ke, ka, ku, kc, cbuf, moh,
+    pts_hbm, rhs_hbm, near_hbm, skel_hbm, top_hbm, x_out, r_out,
+    rhs_in, near, skel_in, top_in, in_s,
+    pts_a, pts_b, pts_c, aux_a, aux_b, aux_c, vals, taug, vb, acc, kq_a, kq_b, kq_c, kd, ke, ka, ku, kc, cbuf, moh,
     zsend, zin, skp, gg, gt, psend, pin, usend, uin, wsend, win, s_one, s_ty, s_tx, s_two,
     pt_s, pt_r, va_s, va_r, z_s, z_r, g_s, g_r, p_s, p_r, u_s, u_r, w_s, w_r, a_s, a_r, b_s, b_r,
 ):
     my_tx = lax.axis_index("tx")
     my_ty = lax.axis_index("ty")
-    pts = (pts_a, pts_b)
-    aux = (aux_a, aux_b)
+    pts = (pts_a, pts_b, pts_c)
+    aux = (aux_a, aux_b, aux_c)
+    kq = (kq_a, kq_b, kq_c)
 
     def tx_at(step):
         return lax.rem(my_tx + (step + N_TX), N_TX)
@@ -150,20 +152,41 @@
         )
         return copy
 
+    def settle(space, sem):
+        pltpu.make_async_copy(space, space, sem).wait()
+
+    def settle_both(space, pair):
+        settle(space, pair[0])
+        settle(space, pair[1])
+
     barrier = pltpu.get_barrier_semaphore()
     for step in range(1, N_TX):
         pl.semaphore_signal(barrier, inc=1, device_id={"tx": tx_at(step)}, device_id_type=pl.DeviceIdType.MESH)
     for step in range(1, N_TY):
         pl.semaphore_signal(barrier, inc=1, device_id={"ty": ty_at(step)}, device_id_type=pl.DeviceIdType.MESH)
-    for half in range(HALVES):
-        vals[0, MINE + half] = rhs_in[half]
+    loads = [
+        pltpu.make_async_copy(near_hbm, near, in_s.at[0]),
+        pltpu.make_async_copy(top_hbm, top_in, in_s.at[1]),
+        pltpu.make_async_copy(skel_hbm, skel_in, in_s.at[2]),
+        pltpu.make_async_copy(rhs_hbm, rhs_in, in_s.at[3]),
+    ]
+    for copy in loads:
+        copy.start()
+    for wave in range(WAVES):
+        for half in range(HALVES):
+            start = half * HALF + STARTS[wave]
+            pltpu.make_async_copy(
+                pts_hbm.at[:, pl.ds(start, PARTS[wave])], pts[wave].at[MINE + half], in_s.at[4 + wave]
+            ).start()
     for half in range(HALVES, 8):
         vals[0, MINE + half] = jnp.zeros((1, HALF), F32)
         vals[1, MINE + half] = jnp.zeros((1, HALF), F32)
+    for copy in loads:
+        copy.wait()
+    for wave in range(WAVES):
+        settle(pts[wave].at[pl.ds(MINE, HALVES)], in_s.at[4 + wave])
     for half in range(HALVES):
-        for wave in range(WAVES):
-            start = half * HALF + wave * PART
-            pts[wave][MINE + half] = pts_in[:, start : start + PART]
+        vals[0, MINE + half] = rhs_in[pl.ds(half * HALF, HALF)].reshape(1, HALF)
 
     remote_gaps = [1, -1, 2, -2]
 
@@ -173,7 +196,7 @@
         place = 8 * (gap + REACH) + 2 * leaf
         return send(
             pts[wave].at[pl.ds(source, 2)], pts[wave].at[pl.ds(place, 2)],
-            pt_s.at[wave, number, leaf], pt_r.at[wave, number, leaf],
+            pt_s.at[wave], pt_r.at[wave, number, leaf] if number < 2 else pt_r.at[wave, 2, 0],
             tx=tx_at(-1 if gap > 0 else 1),
         )
 
@@ -189,29 +212,24 @@
     def pass_on(wave, leaf):
         for number in range(2):
             points_out[wave, leaf, number].wait_recv()
-            copy = point_copy(wave, leaf, number + 2)
-            copy.start()
-            points_out[wave, leaf, number + 2] = copy
+            point_copy(wave, leaf, number + 2).start()
 
     def points_here(wave):
-        for leaf in range(LDEV):
-            for number in range(4):
-                copy = points_out[wave, leaf, number]
-                if number >= 2:
-                    copy.wait_recv()
-                copy.wait_send()
+        settle(pts[wave].at[pl.ds(0, 2 * HALVES)], pt_r.at[wave, 2, 0])
+
+    def points_gone(wave):
+        settle(pts[wave].at[pl.ds(0, 4 * HALVES)], pt_s.at[wave])
 
     def send_values(it):
-        copies = []
-        for number, gap in enumerate(remote_gaps):
+        for gap in remote_gaps:
             place = 8 * (gap + REACH)
-            copy = send(
-                vals.at[it, pl.ds(MINE, 8)], vals.at[it, pl.ds(place, 8)],
-                va_s.at[it, number], va_r.at[it, number], tx=tx_at(-gap),
-            )
-            copy.start()
-            copies.append(copy)
-        return copies
+            send(
+                vals.at[it, pl.ds(MINE, 8)], vals.at[it, pl.ds(place, 8)], va_s.at[it], va_r.at[it], tx=tx_at(-gap)
+            ).start()
+
+    def values_here(it):
+        four = vals.at[it, pl.ds(0, 8 * (GAPS - 1))]
+        settle_both(four, (va_s.at[it], va_r.at[it]))
 
     def slot(leaf, number, half):
         named = near[leaf, number]
@@ -227,9 +245,6 @@
         index = jnp.where(use, 8 * place + 2 * other + other_half, MINE)
         return index, jnp.where(use, 1.0, 0.0), jnp.where(live, 1.0, 0.0) + jnp.where(itself, 1.0, 0.0)
 
-    def split_quad(quad):
-        return lax.div(quad, 2 * SLOTS), lax.rem(lax.div(quad, 2), SLOTS), lax.rem(quad, 2)
-
     def degree(leaf):
         total = 0.0
         for number in range(SLOTS):
@@ -239,11 +254,13 @@
     sub = lax.broadcasted_iota(jnp.int32, (ROWS, 128), 0)
     lane = lax.broadcasted_iota(jnp.int32, (ROWS, 128), 1)
 
-    def mark(quad, table):
-        index, use, unused = slot(*split_quad(quad))
-        return jnp.where((lane == quad) & (sub == index), use, table)
-
-    table = lax.fori_loop(0, QUADS, mark, jnp.zeros((ROWS, 128), F32))
+    def mark(row, table):
+        for number in range(SLOTS):
+            index, use, unused = slot(lax.div(row, 2), number, lax.rem(row, 2))
+            table = jnp.where((lane == 8 * row + number) & (sub == index), use, table)
+        return table
+
+    table = lax.fori_loop(0, HALVES, mark, jnp.zeros((ROWS, 128), F32))
     for leaf in range(LDEV):
         table = jnp.where((lane == QUADS + leaf) & (sub == MINE + 2 * leaf + 1), degree(leaf), table)
     moh[...] = table
@@ -276,19 +293,13 @@
     gg[my_ty] = mine_top
     gt[my_tx] = mine_top
 
-    def send_top():
-        near_copies, far_copies = [], []
+    def send_top_near():
         for step in range(1, N_TY):
-            copy = send(gg.at[my_ty], gg.at[my_ty], g_s.at[step], g_r.at[step], ty=ty_at(step))
-            copy.start()
-            near_copies.append(copy)
+            send(gg.at[my_ty], gg.at[my_ty], g_s.at[0], g_r.at[0], ty=ty_at(step)).start()
+
+    def send_top_far():
         for step in range(1, N_TX):
-            copy = send(gt.at[my_tx], gt.at[my_tx], g_s.at[N_TY + step], g_r.at[N_TY + step], tx=tx_at(step))
-            copy.start()
-            far_copies.append(copy)
-        return near_copies, far_copies
-
-    lax.fori_loop(0, HALVES, own_forms, 0)
+            send(gt.at[my_tx], gt.at[my_tx], g_s.at[1], g_r.at[1], tx=tx_at(step)).start()
 
     def spread(it):
         def step(half, carry):
@@ -324,29 +335,19 @@
             if shift:
                 tile = pltpu.roll(tile, shift, 1)
             psend[it, part] = jnp.where(narrow < TSK, tile, 0.0)
-        out = []
         pin[it, my_ty] = psend[it, my_ty]
         for step in range(1, N_TY):
-            copy = send(psend.at[it, ty_at(step)], pin.at[it, my_ty], p_s.at[it, step], p_r.at[it, step], ty=ty_at(step))
-            copy.start()
-            out.append(copy)
-        return out
-
-    def over_top(it, waiting):
-        for copy in waiting:
-            copy.wait()
+            send(psend.at[it, ty_at(step)], pin.at[it, my_ty], p_s.at[it], p_r.at[it], ty=ty_at(step)).start()
+
+    def over_top(it):
+        settle_both(pin.at[it, pl.ds(0, N_TY - 1)], (p_s.at[it], p_r.at[it]))
         usend[it] = jnp.sum(pin[it], axis=0)
         uin[it, my_tx] = usend[it]
-        out = []
         for step in range(1, N_TX):
-            copy = send(usend.at[it], uin.at[it, my_tx], u_s.at[it, step], u_r.at[it, step], tx=tx_at(step))
-            copy.start()
-            out.append(copy)
-        return out
-
-    def across(it, waiting):
-        for copy in waiting:
-            copy.wait()
+            send(usend.at[it], uin.at[it, my_tx], u_s.at[it], u_r.at[it], tx=tx_at(step)).start()
+
+    def across(it):
+        settle_both(uin.at[it, pl.ds(0, N_TX - 1)], (u_s.at[it], u_r.at[it]))
         tiles = []
         for tile in range(4):
             total = uin[it, 4 * tile]
@@ -356,16 +357,11 @@
         upper = jnp.concatenate(tiles, axis=1)
         wsend[it] = to_row(fold_lanes(kc[...] * upper)) * E_TOP
         win[it, my_ty] = wsend[it]
-        out = []
         for step in range(1, N_TY):
-            copy = send(wsend.at[it], win.at[it, my_ty], w_s.at[it, step], w_r.at[it, step], ty=ty_at(step))
-            copy.start()
-            out.append(copy)
-        return out
-
-    def down(it, waiting):
-        for copy in waiting:
-            copy.wait()
+            send(wsend.at[it], win.at[it, my_ty], w_s.at[it], w_r.at[it], ty=ty_at(step)).start()
+
+    def down(it):
+        settle_both(win.at[it, pl.ds(0, N_TY - 1)], (w_s.at[it], w_r.at[it]))
         middle = to_column(jnp.sum(win[it], axis=0))
         lower = fold_rows(ku[...] * tile_lanes(middle, LDEV * SKEL))
         lower = jnp.sum(lower, axis=0, keepdims=True) * (E_GROUP * A_LEAF * FAR * SLOTS)
@@ -415,6 +411,8 @@
         lax.fori_loop(0, LDEV, step, 0)
 
     def slots(it, wave, start, stop):
+        part = PARTS[wave]
+
         def step(row, carry):
             leaf, half = lax.div(row, 2), lax.rem(row, 2)
             forms, values = [], []
@@ -422,12 +420,12 @@
                 index, use, unused = slot(leaf, number, half)
                 if it == 0:
                     forms.append(form_of(wave, index))
-                values.append(vals[it, index][:, wave * PART : (wave + 1) * PART] * use)
+                values.append(vals[it, index][:, STARTS[wave] : STARTS[wave] + PARTS[wave]] * use)
             form = jnp.concatenate(forms, axis=1) if it == 0 else None
-            total = stretch(it, kq.at[wave, row], row, form, jnp.concatenate(values, axis=1), False, 0)
-            for number in range(SLOTS):
-                place = 2 * SLOTS * leaf + 2 * number + half
-                cbuf[pl.ds(place, 1), wave * PART : (wave + 1) * PART] = total[:, number * PART : (number + 1) * PART]
+            total = stretch(it, kq[wave].at[row], row, form, jnp.concatenate(values, axis=1), False, 0)
+            rows = [total[:, number * part : (number + 1) * part] for number in range(SLOTS)]
+            rows.append(jnp.zeros((8 - SLOTS, part), F32))
+            cbuf[pl.ds(pl.multiple_of(8 * row, 8), 8), STARTS[wave] : STARTS[wave] + part] = jnp.concatenate(rows, axis=0)
             return carry
         lax.fori_loop(start, stop, step, 0)
 
@@ -435,28 +433,16 @@
         parts = jnp.dot(moh[...], cbuf[...], precision=HI, preferred_element_type=F32)
         for place in range(GAPS):
             zsend[it, place] = parts[8 * place : 8 * place + 8]
-        out = []
-        for number, gap in enumerate(remote_gaps):
-            copy = send(
-                zsend.at[it, gap + REACH], zin.at[it, REACH - gap], z_s.at[it, number], z_r.at[it, number], tx=tx_at(gap)
-            )
-            copy.start()
-            out.append(copy)
-        return out
+        for gap in remote_gaps:
+            send(zsend.at[it, gap + REACH], zin.at[it, REACH - gap], z_s.at[it], z_r.at[it], tx=tx_at(gap)).start()
 
     def near_rows(it):
         rows = [to_row(acc[half]) for half in range(HALVES)]
         own = jnp.concatenate(rows + [jnp.zeros((8 - HALVES, HALF), F32)], axis=0)
-        given = jnp.zeros((1, 1), F32)
-        for place in range(GAPS):
-            if place != REACH:
-                theirs = jnp.concatenate([vals[it, 8 * place + half] for half in range(8)], axis=0)
-                given = given + dot(zsend[it, place], theirs)
-        return (own + zsend[it, REACH]) * (1.0 / SLOTS), given * (1.0 / SLOTS)
-
-    def near_back(it, waiting):
-        for copy in waiting:
-            copy.wait()
+        return (own + zsend[it, REACH]) * (1.0 / SLOTS)
+
+    def near_back(it):
+        settle_both(zin.at[it, pl.ds(0, GAPS - 1)], (z_s.at[it], z_r.at[it]))
         total = zin[it, 0]
         for place in range(1, GAPS):
             if place != REACH:
@@ -475,63 +461,24 @@
     def sum_first(number, row):
         s_one[number] = row
         s_ty[number, my_ty] = row
-        out = []
         for step in range(1, N_TY):
-            copy = send(s_one.at[number], s_ty.at[number, my_ty], a_s.at[number, step], a_r.at[number, step], ty=ty_at(step))
-            copy.start()
-            out.append(copy)
-        return out
-
-    def sum_second(number, waiting):
-        for copy in waiting:
-            copy.wait()
+            send(s_one.at[number], s_ty.at[number, my_ty], a_s.at[number], a_r.at[number], ty=ty_at(step)).start()
+
+    def sum_second(number):
+        settle_both(s_ty.at[number, pl.ds(0, N_TY - 1)], (a_s.at[number], a_r.at[number]))
         row = jnp.sum(s_ty[number], axis=0)
         s_two[number] = row
         s_tx[number, my_tx] = row
-        out = []
         for step in range(1, N_TX):
-            copy = send(s_two.at[number], s_tx.at[number, my_tx], b_s.at[number, step], b_r.at[number, step], tx=tx_at(step))
-            copy.start()
-            out.append(copy)
-        return out
-
-    def sum_last(number, waiting, count):
-        for copy in waiting:
-            copy.wait()
+            send(s_two.at[number], s_tx.at[number, my_tx], b_s.at[number], b_r.at[number], tx=tx_at(step)).start()
+
+    def sum_last(number, count):
+        settle_both(s_tx.at[number, pl.ds(0, N_TX - 1)], (b_s.at[number], b_r.at[number]))
         row = jnp.sum(s_tx[number], axis=0)
         return [jnp.sum(jnp.where(narrow == k, row, 0.0), axis=1, keepdims=True) for k in range(count)]
 
     def dot(one, two):
         return jnp.sum(jnp.sum(one * two, axis=0, keepdims=True), axis=1, keepdims=True)
-
-    lax.fori_loop(0, HALVES, own_forms, 0)
-    spread(0)
-    weights = up_leaf(0)
-    start = own_rows(0)
-    pl.semaphore_wait(barrier, N_TX - 1 + N_TY - 1)
-
-    group_near, group_far = send_top()
-    values_out = send_values(0)
-    send_points(0)
-    diagonal(0)
-    for copy in group_near:
-        copy.wait()
-    group_targets = row_targets(gg[...].reshape(GSKEL, 128))
-    for leaf in range(LDEV):
-        ku[:, leaf * SKEL : (leaf + 1) * SKEL] = jnp.exp2(
-            jnp.dot(group_targets, skeleton_form(leaf), preferred_element_type=F32)
-        )
-    flight = up_group(0, weights)
-    for leaf in range(LDEV):
-        pass_on(0, leaf)
-    send_points(1)
-    for copy in group_far:
-        copy.wait()
-    group_sources = row_sources(gt[...].reshape(N_TX * TSK, 128))
-    kc[...] = jnp.exp2(
-        lax.dot_general(group_targets, group_sources, (((1,), (1,)), ((), ())), preferred_element_type=F32)
-    )
-    flight = over_top(0, flight)
 
     def remote_aux(wave):
         for place in range(GAPS):
@@ -541,81 +488,115 @@
                     return carry
                 lax.fori_loop(0, HALVES, one, 0)
 
+    lax.fori_loop(0, HALVES, own_forms, 0)
+    spread(0)
+    start = own_rows(0)
+    pl.semaphore_wait(barrier, N_TX - 1 + N_TY - 1)
+
+    send_points(0)
+    send_top_near()
+    send_points(1)
+    send_top_far()
+    send_values(0)
+    weights = up_leaf(0)
+    settle_both(gg.at[pl.ds(0, N_TY - 1)], (g_s.at[0], g_r.at[0]))
+    group_targets = row_targets(gg[...].reshape(GSKEL, 128))
+    pass_on(0, 0)
+    for leaf in range(LDEV):
+        ku[:, leaf * SKEL : (leaf + 1) * SKEL] = jnp.exp2(
+            jnp.dot(group_targets, skeleton_form(leaf), preferred_element_type=F32)
+        )
+    up_group(0, weights)
+    pass_on(0, 1)
+    pass_on(0, 2)
+    send_points(2)
+    diagonal(0)
+    for leaf in range(LDEV):
+        pass_on(1, leaf)
+    settle_both(gt.at[pl.ds(0, N_TX - 1)], (g_s.at[1], g_r.at[1]))
+    group_sources = row_sources(gt[...].reshape(N_TX * TSK, 128))
+    kc[...] = jnp.exp2(
+        lax.dot_general(group_targets, group_sources, (((1,), (1,)), ((), ())), preferred_element_type=F32)
+    )
+    over_top(0)
+    values_here(0)
     points_here(0)
     remote_aux(0)
-    for copy in values_out:
-        copy.wait()
-    slots(0, 0, 0, 2)
-    pass_on(1, 0)
-    flight = across(0, flight)
-    slots(0, 0, 2, 4)
-    pass_on(1, 1)
-    slots(0, 0, 4, 6)
-    pass_on(1, 2)
-    down(0, flight)
+    slots(0, 0, 0, 1)
+    for leaf in range(LDEV):
+        pass_on(2, leaf)
+    slots(0, 0, 1, HALVES)
+    across(0)
     points_here(1)
     remote_aux(1)
     slots(0, 1, 0, HALVES)
-    back = send_back(0)
-    partial, given = near_rows(0)
-    local = start + partial
-    sums = sum_first(0, pack(dot(start, start), dot(start, local) + given))
-    first = local + near_back(0, back)
+    points_here(2)
+    remote_aux(2)
+    slots(0, 2, 0, HALVES)
+    send_back(0)
+    down(0)
+    first = start + near_rows(0) + near_back(0)
     for half in range(HALVES):
         vals[1, MINE + half] = first[half : half + 1]
 
-    values_out = send_values(1)
+    for wave in range(WAVES):
+        points_gone(wave)
+
+    send_values(1)
+    sum_first(0, pack(dot(start, start), dot(start, first), dot(first, first)))
     spread(1)
-    flight = up_group(1, up_leaf(1))
-    sums = sum_second(0, sums)
+    up_group(1, up_leaf(1))
     diagonal(1)
-    flight = over_top(1, flight)
-    norm, curve = sum_last(0, sums, 2)
+    values_here(1)
+    sum_second(0)
+    slots(1, 0, 0, 1)
+    over_top(1)
+    slots(1, 0, 1, HALVES)
+    slots(1, 1, 0, HALVES)
+    slots(1, 2, 0, HALVES)
+    send_back(1)
+    norm, curve, square = sum_last(0, 3)
     alpha = norm / curve
+    beta = (alpha * alpha * square - norm) / norm
     left = start - alpha * first
-    sums = sum_first(1, pack(dot(left, left)))
-    for copy in values_out:
-        copy.wait()
-    slots(1, 0, 0, HALVES)
-    sums = sum_second(1, sums)
-    flight = across(1, flight)
-    slots(1, 1, 0, HALVES)
-    back = send_back(1)
-    down(1, flight)
-    partial, given = near_rows(1)
-    second = first + partial + near_back(1, back)
-    (norm_next,) = sum_last(1, sums, 1)
-    beta = norm_next / norm
     direction = left + beta * start
+    across(1)
+    down(1)
+    second = first + near_rows(1) + near_back(1)
     image = (1.0 + beta) * first - alpha * second
-    sums = sum_first(2, pack(dot(direction, image)))
-    sums = sum_second(2, sums)
-    (curve,) = sum_last(2, sums, 1)
+    sum_first(1, pack(dot(direction, image), dot(left, left)))
+    sum_second(1)
+    curve, norm_next = sum_last(1, 2)
     step = norm_next / curve
-    x_out[...] = (alpha * start + step * direction)[0:HALVES]
-    r_out[...] = (left - step * image)[0:HALVES]
+    x_rows = alpha * start + step * direction
+    r_rows = left - step * image
+    for half in range(HALVES):
+        x_out[pl.ds(half * HALF, HALF)] = x_rows[half]
+        r_out[pl.ds(half * HALF, HALF)] = r_rows[half]
 
 
 def on_device(points, right_side, near_list, leaf_skeleton, top_index):
     vmem = pl.BlockSpec(memory_space=pltpu.VMEM)
-    smem = pl.BlockSpec(memory_space=pltpu.SMEM)
     dma = pltpu.SemaphoreType.DMA
-    out = jax.ShapeDtypeStruct((HALVES, HALF), F32)
+    out = jax.ShapeDtypeStruct((HALVES * HALF,), F32)
     solution_field, residual = pl.pallas_call(
         body,
         out_shape=(out, out),
-        in_specs=[vmem, vmem, smem, vmem, smem],
+        in_specs=[pl.BlockSpec(memory_space=pl.ANY)] * 5,
         out_specs=(vmem, vmem),
         scratch_shapes=[
-            pltpu.VMEM((ROWS, D, PART), BF16),
-            pltpu.VMEM((ROWS, D, PART), BF16),
-            pltpu.VMEM((ROWS, 16, PART), BF16),
-            pltpu.VMEM((ROWS, 16, PART), BF16),
+            pltpu.VMEM((HALVES * HALF,), F32),
+            pltpu.SMEM((LDEV, SLOTS), jnp.int32),
+            pltpu.VMEM((LDEV, SKEL), jnp.int32),
+            pltpu.SMEM((TSK,), jnp.int32),
+            dma((4 + WAVES,)),
+            *[pltpu.VMEM((ROWS, D, part), BF16) for part in PARTS],
+            *[pltpu.VMEM((ROWS, 16, part), BF16) for part in PARTS],
             pltpu.VMEM((2, ROWS, 1, HALF), F32),
             pltpu.VMEM((HALVES, HALF, 256), BF16),
             pltpu.VMEM((HALVES, HALF, 128), F32),
             pltpu.VMEM((HALVES, HALF, 128), F32),
-            pltpu.VMEM((WAVES, HALVES, HALF, WIDE), F32),
+            *[pltpu.VMEM((HALVES, HALF, SLOTS * part), F32) for part in PARTS],
             pltpu.VMEM((LDEV, HALF, LEAF), F32),
             pltpu.VMEM((LDEV, HALF, HALF), F32),
             pltpu.VMEM((HALVES, HALF, SKEL), F32),
@@ -634,26 +615,19 @@
             pltpu.VMEM((2, N_TX, 1, 128), F32),
             pltpu.VMEM((2, 1, GSKEL), F32),
             pltpu.VMEM((2, N_TY, 1, GSKEL), F32),
-            pltpu.VMEM((3, 1, 128), F32),
-            pltpu.VMEM((3, N_TY, 1, 128), F32),
-            pltpu.VMEM((3, N_TX, 1, 128), F32),
-            pltpu.VMEM((3, 1, 128), F32),
-            dma((WAVES, 4, LDEV)), dma((WAVES, 4, LDEV)),
-            dma((2, 4)), dma((2, 4)),
-            dma((2, 4)), dma((2, 4)),
-            dma((N_TX + N_TY,)), dma((N_TX + N_TY,)),
-            dma((2, N_TY)), dma((2, N_TY)),
-            dma((2, N_TX)), dma((2, N_TX)),
-            dma((2, N_TY)), dma((2, N_TY)),
-            dma((3, N_TY)), dma((3, N_TY)),
-            dma((3, N_TX)), dma((3, N_TX)),
+            pltpu.VMEM((2, 1, 128), F32),
+            pltpu.VMEM((2, N_TY, 1, 128), F32),
+            pltpu.VMEM((2, N_TX, 1, 128), F32),
+            pltpu.VMEM((2, 1, 128), F32),
+            dma((WAVES,)), dma((WAVES, 3, LDEV)),
+            *[dma((2,))] * 16,
         ],
         compiler_params=pltpu.CompilerParams(
             collective_id=0, has_side_effects=True, vmem_limit_bytes=64 * 1024 * 1024 - 512 * 1024
         ),
         name="ridge_cg",
-    )(points, right_side.reshape(HALVES, 1, HALF), near_list, leaf_skeleton, top_index)
-    return solution_field.reshape(-1), residual.reshape(-1)
+    )(points, right_side, near_list, leaf_skeleton, top_index)
+    return solution_field, residual
 
 
 def solution(mesh):

time: 86.6 us -> 74.1 us (0.86)
  Pallas kernels: 83.8 us -> 71.3 us
    pallas_call x1, Pallas kernels: 83.8 us -> 71.3 us  [on_device(): pl.pallas_call(body, out_shape=(out, out), in_specs=[pl.BlockSpec(memory_...]
    reshape x2 -> x0, local copies, waits for them, and re-layouts: 1.93 us -> none  [on_device(): return (solution_field.reshape(-1), residual.reshape(-1))]
    unnamed x2 -> x4, local copies, waits for them, and re-layouts: 0.01 us -> 1.92 us
where the time goes in v3:
time: 74.1 us; the launch traced here: 73.9 us
  Pallas kernels  71.3 us (96%)
  local copies, waits for them, and re-layouts  1.92 us (3%)
    pallas_call x1, Pallas kernels, on_device(): pl.pallas_call(body, out_shape=(out, out), in_specs=[pl.BlockSpec(memory_...  71.3 us
    unnamed x4, local copies, waits for them, and re-layouts  1.92 us

profile of v3, /device:TPU:0, one launch (start us, length us, event | category | flops | bytes accessed | tf_op | source)
XLA Modules:
  0.0 73.9 jit_solution(17426501063934777261)
XLA Ops:
  0.6 71.3 %ridge_cg.1 = (f32[3072]{0:T(1024)}, f32[3072]{0:T(1024)}) custom-call(bf16[64,3072]{1,0:T(8,128)(2,1)} %pts_hbm.1, f32[3072]{0:T(1024)} %rhs_hbm.1, s32[3,6]{1,0:T(4,128)} %near_hbm.1, s32[3,256]{1,0:T(4,128)} %skel_hbm.1, s32[32]{0:T(128)} %top_hbm.1), custom_call_target="tpu_custom_call" | custom-call | tf_op jit(solution)/shard_map/ridge_cg/pallas_call | solution.py:582
  71.9 0.0 copy-start
  72.0 1.3 %copy.9 = f32[3072]{0:T(1024)} copy(f32[3072]{0:T(1024)} %get-tuple-element.4) | data formatting | bytes 24576
  73.3 0.0 copy-done
  73.3 0.6 copy.10
Async XLA Ops:
  71.9 1.3 %copy-start = (f32[3072]{0:T(1024)S(1)}, f32[3072]{0:T(1024)}, u32[]{:S(2)}) copy-start(f32[3072]{0:T(1024)} %get-tuple-element.5) | copy-start | bytes 36868

commit v4 on v3

--- a/solution.py
+++ b/solution.py
@@ -97,9 +97,10 @@
 
 
 def to_row(columns):
-    ones = jnp.ones((8, 128), F32)
+    ones = jnp.ones((8, 384), BF16)
+    parts = jnp.concatenate(split3(columns), axis=1)
     return lax.dot_general(
-        ones, columns, (((1,), (1,)), ((), ())), precision=HI, preferred_element_type=F32
+        ones, parts, (((1,), (1,)), ((), ())), preferred_element_type=F32
     )[0:1]
 
 
@@ -130,7 +131,7 @@
     pts_hbm, rhs_hbm, near_hbm, skel_hbm, top_hbm, x_out, r_out,
     rhs_in, near, skel_in, top_in, in_s,
     pts_a, pts_b, pts_c, aux_a, aux_b, aux_c, vals, taug, vb, acc, kq_a, kq_b, kq_c, kd, ke, ka, ku, kc, cbuf, moh,
-    zsend, zin, skp, gg, gt, psend, pin, usend, uin, wsend, win, s_one, s_ty, s_tx, s_two,
+    zsend, zin, skp, gg, gt, psend, pin, ufull, usend, uin, wsend, win, s_one, s_ty, s_tx, s_two,
     pt_s, pt_r, va_s, va_r, z_s, z_r, g_s, g_r, p_s, p_r, u_s, u_r, w_s, w_r, a_s, a_r, b_s, b_r,
 ):
     my_tx = lax.axis_index("tx")
@@ -327,21 +328,28 @@
 
     narrow = lax.broadcasted_iota(jnp.int32, (1, 128), 1)
 
-    def up_group(it, weights):
-        partial = to_row(fold_lanes(ku[...] * weights)) * E_GROUP
+    def by_part(row):
+        rows = []
         for part in range(N_TY):
-            tile = partial[:, 128 * (part // 4) : 128 * (part // 4) + 128]
+            tile = row[:, 128 * (part // 4) : 128 * (part // 4) + 128]
             shift = (128 - TSK * (part % 4)) % 128
             if shift:
                 tile = pltpu.roll(tile, shift, 1)
-            psend[it, part] = jnp.where(narrow < TSK, tile, 0.0)
-        pin[it, my_ty] = psend[it, my_ty]
+            rows.append(jnp.where(narrow < TSK, tile, 0.0))
+        return rows
+
+    def up_group(it, weights):
+        partial = to_row(fold_lanes(ku[...] * weights)) * E_GROUP
+        for part, row in enumerate(by_part(partial)):
+            psend[it, part] = row
+            pin[it, my_ty, part] = row
         for step in range(1, N_TY):
-            send(psend.at[it, ty_at(step)], pin.at[it, my_ty], p_s.at[it], p_r.at[it], ty=ty_at(step)).start()
+            send(psend.at[it], pin.at[it, my_ty], p_s.at[it], p_r.at[it], ty=ty_at(step)).start()
 
     def over_top(it):
         settle_both(pin.at[it, pl.ds(0, N_TY - 1)], (p_s.at[it], p_r.at[it]))
-        usend[it] = jnp.sum(pin[it], axis=0)
+        ufull[it] = jnp.sum(pin[it], axis=0)
+        usend[it] = ufull[it, my_ty]
         uin[it, my_tx] = usend[it]
         for step in range(1, N_TX):
             send(usend.at[it], uin.at[it, my_tx], u_s.at[it], u_r.at[it], tx=tx_at(step)).start()
@@ -369,7 +377,7 @@
             weights = lower[:, leaf * SKEL : (leaf + 1) * SKEL]
             for half in range(2):
                 row = 2 * leaf + half
-                acc[row] += fold_lanes(ka[row] * weights)
+                acc[row] = fold_lanes(ka[row] * weights)
 
     def stretch(it, store, row, form, values, fresh, first):
         width = values.shape[1]
@@ -436,10 +444,12 @@
         for gap in remote_gaps:
             send(zsend.at[it, gap + REACH], zin.at[it, REACH - gap], z_s.at[it], z_r.at[it], tx=tx_at(gap)).start()
 
+    def rows_of_acc():
+        rows = [to_row(acc[half]) for half in range(HALVES)]
+        return jnp.concatenate(rows + [jnp.zeros((8 - HALVES, HALF), F32)], axis=0) * (1.0 / SLOTS)
+
     def near_rows(it):
-        rows = [to_row(acc[half]) for half in range(HALVES)]
-        own = jnp.concatenate(rows + [jnp.zeros((8 - HALVES, HALF), F32)], axis=0)
-        return (own + zsend[it, REACH]) * (1.0 / SLOTS)
+        return rows_of_acc() + zsend[it, REACH] * (1.0 / SLOTS)
 
     def near_back(it):
         settle_both(zin.at[it, pl.ds(0, GAPS - 1)], (z_s.at[it], z_r.at[it]))
@@ -477,8 +487,11 @@
         row = jnp.sum(s_tx[number], axis=0)
         return [jnp.sum(jnp.where(narrow == k, row, 0.0), axis=1, keepdims=True) for k in range(count)]
 
+    def total_of(tile):
+        return jnp.sum(jnp.sum(tile, axis=0, keepdims=True), axis=1, keepdims=True)
+
     def dot(one, two):
-        return jnp.sum(jnp.sum(one * two, axis=0, keepdims=True), axis=1, keepdims=True)
+        return total_of(one * two)
 
     def remote_aux(wave):
         for place in range(GAPS):
@@ -534,8 +547,9 @@
     remote_aux(2)
     slots(0, 2, 0, HALVES)
     send_back(0)
+    own_first = start + near_rows(0)
     down(0)
-    first = start + near_rows(0) + near_back(0)
+    first = own_first + rows_of_acc() + near_back(0)
     for half in range(HALVES):
         vals[1, MINE + half] = first[half : half + 1]
 
@@ -549,23 +563,40 @@
     diagonal(1)
     values_here(1)
     sum_second(0)
-    slots(1, 0, 0, 1)
+    slots(1, 0, 0, 2)
     over_top(1)
-    slots(1, 0, 1, HALVES)
+    slots(1, 0, 2, HALVES)
     slots(1, 1, 0, HALVES)
     slots(1, 2, 0, HALVES)
     send_back(1)
+    own_second = first + near_rows(1)
     norm, curve, square = sum_last(0, 3)
     alpha = norm / curve
     beta = (alpha * alpha * square - norm) / norm
     left = start - alpha * first
     direction = left + beta * start
     across(1)
+    c_start, c_first = 1.0 + beta, -alpha
+    bend = dot(direction, c_start * own_first + c_first * own_second)
+    given = jnp.zeros((8, HALF), F32)
+    for place in range(GAPS):
+        if place != REACH:
+            theirs = [
+                jnp.concatenate([vals[it, 8 * place + half] for half in range(8)], axis=0) for it in range(2)
+            ]
+            given = given + (c_start * theirs[0] + c_first * theirs[1]) * (
+                c_start * zsend[0, place] + c_first * zsend[1, place]
+            )
+    top = jnp.zeros((1, 128), F32)
+    for part, row in enumerate(by_part(c_start * wsend[0] + c_first * wsend[1])):
+        top = top + row * (c_start * ufull[0, part] + c_first * ufull[1, part])
+    bend = bend + total_of(given) * (1.0 / SLOTS) + total_of(top) * FAR
+    sum_first(1, pack(bend, dot(left, left)))
     down(1)
-    second = first + near_rows(1) + near_back(1)
-    image = (1.0 + beta) * first - alpha * second
-    sum_first(1, pack(dot(direction, image), dot(left, left)))
+    far_second = rows_of_acc()
     sum_second(1)
+    second = own_second + far_second + near_back(1)
+    image = c_start * first + c_first * second
     curve, norm_next = sum_last(1, 2)
     step = norm_next / curve
     x_rows = alpha * start + step * direction
@@ -610,6 +641,7 @@
             pltpu.VMEM((N_TY, TSK, 128), BF16),
             pltpu.VMEM((N_TX, TSK, 128), BF16),
             pltpu.VMEM((2, N_TY, 1, 128), F32),
+            pltpu.VMEM((2, N_TY, N_TY, 1, 128), F32),
             pltpu.VMEM((2, N_TY, 1, 128), F32),
             pltpu.VMEM((2, 1, 128), F32),
             pltpu.VMEM((2, N_TX, 1, 128), F32),

time: 74.1 us -> 69.8 us (0.942)
  Pallas kernels: 71.3 us -> 66.9 us
    pallas_call x1, Pallas kernels: 71.3 us -> 66.9 us  [on_device(): pl.pallas_call(body, out_shape=(out, out), in_specs=[pl.BlockSpec(memory_...]
where the time goes in v4:
time: 69.8 us; the launch traced here: 69.5 us
  Pallas kernels  66.9 us (96%)
  local copies, waits for them, and re-layouts  1.92 us (3%)
    pallas_call x1, Pallas kernels, on_device(): pl.pallas_call(body, out_shape=(out, out), in_specs=[pl.BlockSpec(memory_...  66.9 us
    unnamed x4, local copies, waits for them, and re-layouts  1.92 us

profile of v4, /device:TPU:0, one launch (start us, length us, event | category | flops | bytes accessed | tf_op | source)
XLA Modules:
  0.0 69.5 jit_solution(7964616475689628652)
XLA Ops:
  0.6 66.9 %ridge_cg.1 = (f32[3072]{0:T(1024)}, f32[3072]{0:T(1024)}) custom-call(bf16[64,3072]{1,0:T(8,128)(2,1)} %pts_hbm.1, f32[3072]{0:T(1024)} %rhs_hbm.1, s32[3,6]{1,0:T(4,128)} %near_hbm.1, s32[3,256]{1,0:T(4,128)} %skel_hbm.1, s32[32]{0:T(128)} %top_hbm.1), custom_call_target="tpu_custom_call" | custom-call | tf_op jit(solution)/shard_map/ridge_cg/pallas_call | solution.py:613
  67.5 0.0 copy-start
  67.5 1.3 %copy.9 = f32[3072]{0:T(1024)} copy(f32[3072]{0:T(1024)} %get-tuple-element.4) | data formatting | bytes 24576
  68.8 0.0 copy-done
  68.9 0.6 copy.10
Async XLA Ops:
  67.5 1.3 %copy-start = (f32[3072]{0:T(1024)S(1)}, f32[3072]{0:T(1024)}, u32[]{:S(2)}) copy-start(f32[3072]{0:T(1024)} %get-tuple-element.5) | copy-start | bytes 36868

commit v5 on v4

--- a/solution.py
+++ b/solution.py
@@ -28,9 +28,10 @@
 ROWS = 8 * GAPS
 MINE = 8 * REACH
 QUADS = 8 * HALVES
+SPARE = 64
 CHUNK = 128
-PARTS = (256, 128, 128)
-STARTS = (0, 256, 384)
+PARTS = (128, 128, 128, 128)
+STARTS = (0, 128, 256, 384)
 WAVES = len(PARTS)
 
 SCALE = 2.0 * math.log2(math.e) / 20.0
@@ -59,6 +60,16 @@
     return parts
 
 
+def aux_of_many(coords):
+    wide = coords.astype(F32)
+    norm = (-0.5 * SCALE) * jnp.sum(wide * wide, axis=1, keepdims=True)
+    high, mid, low = [t.astype(F32) for t in split3(norm)]
+    row = lax.broadcasted_iota(jnp.int32, (coords.shape[0], 16, coords.shape[2]), 1)
+    ones = jnp.where(row < 3, 1.0, 0.0)
+    parts = jnp.where(row == 3, high, jnp.where(row == 4, mid, jnp.where(row == 5, low, ones)))
+    return parts.astype(BF16)
+
+
 def source_form(coords, aux):
     pad = jnp.zeros((48, coords.shape[1]), BF16)
     return jnp.concatenate([coords, coords, coords, aux, pad], axis=0)
@@ -130,15 +141,15 @@
 def body(
     pts_hbm, rhs_hbm, near_hbm, skel_hbm, top_hbm, x_out, r_out,
     rhs_in, near, skel_in, top_in, in_s,
-    pts_a, pts_b, pts_c, aux_a, aux_b, aux_c, vals, taug, vb, acc, kq_a, kq_b, kq_c, kd, ke, ka, ku, kc, cbuf, moh,
+    pts_a, pts_b, pts_c, pts_d, aux_a, aux_b, aux_c, aux_d, vals, taug, vb, acc, kq_a, kq_b, kq_c, kq_d, kd, ke, ka, ku, kc, cbuf, moh,
     zsend, zin, skp, gg, gt, psend, pin, ufull, usend, uin, wsend, win, s_one, s_ty, s_tx, s_two,
     pt_s, pt_r, va_s, va_r, z_s, z_r, g_s, g_r, p_s, p_r, u_s, u_r, w_s, w_r, a_s, a_r, b_s, b_r,
 ):
     my_tx = lax.axis_index("tx")
     my_ty = lax.axis_index("ty")
-    pts = (pts_a, pts_b, pts_c)
-    aux = (aux_a, aux_b, aux_c)
-    kq = (kq_a, kq_b, kq_c)
+    pts = (pts_a, pts_b, pts_c, pts_d)
+    aux = (aux_a, aux_b, aux_c, aux_d)
+    kq = (kq_a, kq_b, kq_c, kq_d)
 
     def tx_at(step):
         return lax.rem(my_tx + (step + N_TX), N_TX)
@@ -191,32 +202,30 @@
 
     remote_gaps = [1, -1, 2, -2]
 
-    def point_copy(wave, leaf, number):
+    def point_copy(wave, number):
         gap = remote_gaps[number]
-        source = 8 * (REACH if number < 2 else REACH + gap // 2) + 2 * leaf
-        place = 8 * (gap + REACH) + 2 * leaf
+        source = 8 * (REACH if number < 2 else REACH + gap // 2)
+        place = 8 * (gap + REACH)
         return send(
-            pts[wave].at[pl.ds(source, 2)], pts[wave].at[pl.ds(place, 2)],
-            pt_s.at[wave], pt_r.at[wave, number, leaf] if number < 2 else pt_r.at[wave, 2, 0],
-            tx=tx_at(-1 if gap > 0 else 1),
+            pts[wave].at[pl.ds(source, HALVES)], pts[wave].at[pl.ds(place, HALVES)],
+            pt_s.at[wave], pt_r.at[wave, min(number, 2)], tx=tx_at(-1 if gap > 0 else 1),
         )
 
     points_out = {}
 
     def send_points(wave):
-        for leaf in range(LDEV):
-            for number in range(2):
-                copy = point_copy(wave, leaf, number)
-                copy.start()
-                points_out[wave, leaf, number] = copy
-
-    def pass_on(wave, leaf):
         for number in range(2):
-            points_out[wave, leaf, number].wait_recv()
-            point_copy(wave, leaf, number + 2).start()
+            copy = point_copy(wave, number)
+            copy.start()
+            points_out[wave, number] = copy
+
+    def pass_on(wave):
+        for number in range(2):
+            points_out[wave, number].wait_recv()
+            point_copy(wave, number + 2).start()
 
     def points_here(wave):
-        settle(pts[wave].at[pl.ds(0, 2 * HALVES)], pt_r.at[wave, 2, 0])
+        settle(pts[wave].at[pl.ds(0, 2 * HALVES)], pt_r.at[wave, 2])
 
     def points_gone(wave):
         settle(pts[wave].at[pl.ds(0, 4 * HALVES)], pt_s.at[wave])
@@ -338,18 +347,20 @@
             rows.append(jnp.where(narrow < TSK, tile, 0.0))
         return rows
 
-    def up_group(it, weights):
+    def up_group(it, weights, extra):
         partial = to_row(fold_lanes(ku[...] * weights)) * E_GROUP
         for part, row in enumerate(by_part(partial)):
             psend[it, part] = row
             pin[it, my_ty, part] = row
+        psend[it, N_TY] = extra
+        pin[it, my_ty, N_TY] = extra
         for step in range(1, N_TY):
             send(psend.at[it], pin.at[it, my_ty], p_s.at[it], p_r.at[it], ty=ty_at(step)).start()
 
     def over_top(it):
         settle_both(pin.at[it, pl.ds(0, N_TY - 1)], (p_s.at[it], p_r.at[it]))
         ufull[it] = jnp.sum(pin[it], axis=0)
-        usend[it] = ufull[it, my_ty]
+        usend[it] = ufull[it, my_ty] + ufull[it, N_TY]
         uin[it, my_tx] = usend[it]
         for step in range(1, N_TX):
             send(usend.at[it], uin.at[it, my_tx], u_s.at[it], u_r.at[it], tx=tx_at(step)).start()
@@ -358,13 +369,15 @@
         settle_both(uin.at[it, pl.ds(0, N_TX - 1)], (u_s.at[it], u_r.at[it]))
         tiles = []
         for tile in range(4):
-            total = uin[it, 4 * tile]
+            total = jnp.where(narrow < TSK, uin[it, 4 * tile], 0.0)
             for k in range(1, 4):
-                total = total + pltpu.roll(uin[it, 4 * tile + k], TSK * k, 1)
+                total = total + pltpu.roll(jnp.where(narrow < TSK, uin[it, 4 * tile + k], 0.0), TSK * k, 1)
             tiles.append(total)
         upper = jnp.concatenate(tiles, axis=1)
         wsend[it] = to_row(fold_lanes(kc[...] * upper)) * E_TOP
         win[it, my_ty] = wsend[it]
+
+    def send_middle(it):
         for step in range(1, N_TY):
             send(wsend.at[it], win.at[it, my_ty], w_s.at[it], w_r.at[it], ty=ty_at(step)).start()
 
@@ -438,7 +451,12 @@
         lax.fori_loop(start, stop, step, 0)
 
     def send_back(it):
-        parts = jnp.dot(moh[...], cbuf[...], precision=HI, preferred_element_type=F32)
+        table = moh[...].astype(BF16)
+        parts = jnp.dot(
+            jnp.concatenate([table] * 3, axis=1),
+            jnp.concatenate(split3(cbuf[...]), axis=0),
+            preferred_element_type=F32,
+        )
         for place in range(GAPS):
             zsend[it, place] = parts[8 * place : 8 * place + 8]
         for gap in remote_gaps:
@@ -465,8 +483,11 @@
     def pack(*sums):
         row = jnp.zeros((1, 128), F32)
         for number, value in enumerate(sums):
-            row = jnp.where(narrow == number, value, row)
+            row = jnp.where(narrow == SPARE + number, value, row)
         return row
+
+    def unpack(row, count):
+        return [jnp.sum(jnp.where(narrow == SPARE + k, row, 0.0), axis=1, keepdims=True) for k in range(count)]
 
     def sum_first(number, row):
         s_one[number] = row
@@ -484,8 +505,7 @@
 
     def sum_last(number, count):
         settle_both(s_tx.at[number, pl.ds(0, N_TX - 1)], (b_s.at[number], b_r.at[number]))
-        row = jnp.sum(s_tx[number], axis=0)
-        return [jnp.sum(jnp.where(narrow == k, row, 0.0), axis=1, keepdims=True) for k in range(count)]
+        return unpack(jnp.sum(s_tx[number], axis=0), count)
 
     def total_of(tile):
         return jnp.sum(jnp.sum(tile, axis=0, keepdims=True), axis=1, keepdims=True)
@@ -496,10 +516,8 @@
     def remote_aux(wave):
         for place in range(GAPS):
             if place != REACH:
-                def one(half, carry, place=place):
-                    aux[wave][8 * place + half] = aux_rows(pts[wave][8 * place + half], False).astype(BF16)
-                    return carry
-                lax.fori_loop(0, HALVES, one, 0)
+                six = pl.ds(8 * place, HALVES)
+                aux[wave][six] = aux_of_many(pts[wave][six])
 
     lax.fori_loop(0, HALVES, own_forms, 0)
     spread(0)
@@ -509,43 +527,45 @@
     send_points(0)
     send_top_near()
     send_points(1)
-    send_top_far()
+    send_points(2)
     send_values(0)
     weights = up_leaf(0)
+    pass_on(0)
+    send_points(3)
+    send_top_far()
     settle_both(gg.at[pl.ds(0, N_TY - 1)], (g_s.at[0], g_r.at[0]))
     group_targets = row_targets(gg[...].reshape(GSKEL, 128))
-    pass_on(0, 0)
     for leaf in range(LDEV):
         ku[:, leaf * SKEL : (leaf + 1) * SKEL] = jnp.exp2(
             jnp.dot(group_targets, skeleton_form(leaf), preferred_element_type=F32)
         )
-    up_group(0, weights)
-    pass_on(0, 1)
-    pass_on(0, 2)
-    send_points(2)
+    up_group(0, weights, jnp.zeros((1, 128), F32))
+    pass_on(1)
     diagonal(0)
-    for leaf in range(LDEV):
-        pass_on(1, leaf)
+    pass_on(2)
+    over_top(0)
+    values_here(0)
+    points_here(0)
+    remote_aux(0)
+    slots(0, 0, 0, 4)
+    pass_on(3)
+    slots(0, 0, 4, HALVES)
+    points_here(1)
+    remote_aux(1)
+    slots(0, 1, 0, HALVES)
     settle_both(gt.at[pl.ds(0, N_TX - 1)], (g_s.at[1], g_r.at[1]))
     group_sources = row_sources(gt[...].reshape(N_TX * TSK, 128))
     kc[...] = jnp.exp2(
         lax.dot_general(group_targets, group_sources, (((1,), (1,)), ((), ())), preferred_element_type=F32)
     )
-    over_top(0)
-    values_here(0)
-    points_here(0)
-    remote_aux(0)
-    slots(0, 0, 0, 1)
-    for leaf in range(LDEV):
-        pass_on(2, leaf)
-    slots(0, 0, 1, HALVES)
     across(0)
-    points_here(1)
-    remote_aux(1)
-    slots(0, 1, 0, HALVES)
+    send_middle(0)
     points_here(2)
     remote_aux(2)
     slots(0, 2, 0, HALVES)
+    points_here(3)
+    remote_aux(3)
+    slots(0, 3, 0, HALVES)
     send_back(0)
     own_first = start + near_rows(0)
     down(0)
@@ -557,25 +577,24 @@
         points_gone(wave)
 
     send_values(1)
-    sum_first(0, pack(dot(start, start), dot(start, first), dot(first, first)))
     spread(1)
-    up_group(1, up_leaf(1))
+    up_group(1, up_leaf(1), pack(dot(start, start), dot(start, first), dot(first, first)))
     diagonal(1)
     values_here(1)
-    sum_second(0)
-    slots(1, 0, 0, 2)
+    slots(1, 0, 0, 3)
     over_top(1)
-    slots(1, 0, 2, HALVES)
+    slots(1, 0, 3, HALVES)
     slots(1, 1, 0, HALVES)
-    slots(1, 2, 0, HALVES)
+    for wave in range(2, WAVES):
+        slots(1, wave, 0, HALVES)
     send_back(1)
     own_second = first + near_rows(1)
-    norm, curve, square = sum_last(0, 3)
+    across(1)
+    norm, curve, square = unpack(jnp.sum(uin[1], axis=0), 3)
     alpha = norm / curve
     beta = (alpha * alpha * square - norm) / norm
     left = start - alpha * first
     direction = left + beta * start
-    across(1)
     c_start, c_first = 1.0 + beta, -alpha
     bend = dot(direction, c_start * own_first + c_first * own_second)
     given = jnp.zeros((8, HALF), F32)
@@ -591,13 +610,15 @@
     for part, row in enumerate(by_part(c_start * wsend[0] + c_first * wsend[1])):
         top = top + row * (c_start * ufull[0, part] + c_first * ufull[1, part])
     bend = bend + total_of(given) * (1.0 / SLOTS) + total_of(top) * FAR
-    sum_first(1, pack(bend, dot(left, left)))
+    sum_first(0, pack(bend, dot(left, left)))
+    send_middle(1)
+    from_others = near_back(1)
+    sum_second(0)
     down(1)
     far_second = rows_of_acc()
-    sum_second(1)
-    second = own_second + far_second + near_back(1)
+    second = own_second + far_second + from_others
     image = c_start * first + c_first * second
-    curve, norm_next = sum_last(1, 2)
+    curve, norm_next = sum_last(0, 2)
     step = norm_next / curve
     x_rows = alpha * start + step * direction
     r_rows = left - step * image
@@ -640,18 +661,18 @@
             pltpu.VMEM((128, LDEV * SKEL), BF16),
             pltpu.VMEM((N_TY, TSK, 128), BF16),
             pltpu.VMEM((N_TX, TSK, 128), BF16),
-            pltpu.VMEM((2, N_TY, 1, 128), F32),
-            pltpu.VMEM((2, N_TY, N_TY, 1, 128), F32),
-            pltpu.VMEM((2, N_TY, 1, 128), F32),
+            pltpu.VMEM((2, N_TY + 1, 1, 128), F32),
+            pltpu.VMEM((2, N_TY, N_TY + 1, 1, 128), F32),
+            pltpu.VMEM((2, N_TY + 1, 1, 128), F32),
             pltpu.VMEM((2, 1, 128), F32),
             pltpu.VMEM((2, N_TX, 1, 128), F32),
             pltpu.VMEM((2, 1, GSKEL), F32),
             pltpu.VMEM((2, N_TY, 1, GSKEL), F32),
-            pltpu.VMEM((2, 1, 128), F32),
-            pltpu.VMEM((2, N_TY, 1, 128), F32),
-            pltpu.VMEM((2, N_TX, 1, 128), F32),
-            pltpu.VMEM((2, 1, 128), F32),
-            dma((WAVES,)), dma((WAVES, 3, LDEV)),
+            pltpu.VMEM((1, 1, 128), F32),
+            pltpu.VMEM((1, N_TY, 1, 128), F32),
+            pltpu.VMEM((1, N_TX, 1, 128), F32),
+            pltpu.VMEM((1, 1, 128), F32),
+            dma((WAVES,)), dma((WAVES, 3)),
             *[dma((2,))] * 16,
         ],
         compiler_params=pltpu.CompilerParams(

time: 69.8 us -> 67.4 us (0.966)
  Pallas kernels: 66.9 us -> 64.6 us
    pallas_call x1, Pallas kernels: 66.9 us -> 64.6 us  [on_device(): pl.pallas_call(body, out_shape=(out, out), in_specs=[pl.BlockSpec(memory_...]
where the time goes in v5:
time: 67.4 us; the launch traced here: 67.2 us
  Pallas kernels  64.6 us (96%)
  local copies, waits for them, and re-layouts  1.92 us (3%)
    pallas_call x1, Pallas kernels, on_device(): pl.pallas_call(body, out_shape=(out, out), in_specs=[pl.BlockSpec(memory_...  64.6 us
    unnamed x4, local copies, waits for them, and re-layouts  1.92 us

profile of v5, /device:TPU:0, one launch (start us, length us, event | category | flops | bytes accessed | tf_op | source)
XLA Modules:
  0.0 67.2 jit_solution(13351789931302934019)
XLA Ops:
  0.6 64.6 %ridge_cg.1 = (f32[3072]{0:T(1024)}, f32[3072]{0:T(1024)}) custom-call(bf16[64,3072]{1,0:T(8,128)(2,1)} %pts_hbm.1, f32[3072]{0:T(1024)} %rhs_hbm.1, s32[3,6]{1,0:T(4,128)} %near_hbm.1, s32[3,256]{1,0:T(4,128)} %skel_hbm.1, s32[32]{0:T(128)} %top_hbm.1), custom_call_target="tpu_custom_call" | custom-call | tf_op jit(solution)/shard_map/ridge_cg/pallas_call | solution.py:634
  65.2 0.0 copy-start
  65.2 1.3 %copy.9 = f32[3072]{0:T(1024)} copy(f32[3072]{0:T(1024)} %get-tuple-element.4) | data formatting | bytes 24576
  66.6 0.0 copy-done
  66.6 0.6 copy.10
Async XLA Ops:
  65.2 1.3 %copy-start = (f32[3072]{0:T(1024)S(1)}, f32[3072]{0:T(1024)}, u32[]{:S(2)}) copy-start(f32[3072]{0:T(1024)} %get-tuple-element.5) | copy-start | bytes 36868

commit v6 on v5

--- a/solution.py
+++ b/solution.py
@@ -139,7 +139,7 @@
 
 
 def body(
-    pts_hbm, rhs_hbm, near_hbm, skel_hbm, top_hbm, x_out, r_out,
+    pts_hbm, rhs_hbm, near_hbm, skel_hbm, top_hbm, out,
     rhs_in, near, skel_in, top_in, in_s,
     pts_a, pts_b, pts_c, pts_d, aux_a, aux_b, aux_c, aux_d, vals, taug, vb, acc, kq_a, kq_b, kq_c, kq_d, kd, ke, ka, ku, kc, cbuf, moh,
     zsend, zin, skp, gg, gt, psend, pin, ufull, usend, uin, wsend, win, s_one, s_ty, s_tx, s_two,
@@ -529,10 +529,9 @@
     send_points(1)
     send_points(2)
     send_values(0)
-    weights = up_leaf(0)
     pass_on(0)
     send_points(3)
-    send_top_far()
+    weights = up_leaf(0)
     settle_both(gg.at[pl.ds(0, N_TY - 1)], (g_s.at[0], g_r.at[0]))
     group_targets = row_targets(gg[...].reshape(GSKEL, 128))
     for leaf in range(LDEV):
@@ -549,10 +548,14 @@
     remote_aux(0)
     slots(0, 0, 0, 4)
     pass_on(3)
+    send_top_far()
     slots(0, 0, 4, HALVES)
     points_here(1)
     remote_aux(1)
     slots(0, 1, 0, HALVES)
+    points_here(2)
+    remote_aux(2)
+    slots(0, 2, 0, HALVES)
     settle_both(gt.at[pl.ds(0, N_TX - 1)], (g_s.at[1], g_r.at[1]))
     group_sources = row_sources(gt[...].reshape(N_TX * TSK, 128))
     kc[...] = jnp.exp2(
@@ -560,9 +563,6 @@
     )
     across(0)
     send_middle(0)
-    points_here(2)
-    remote_aux(2)
-    slots(0, 2, 0, HALVES)
     points_here(3)
     remote_aux(3)
     slots(0, 3, 0, HALVES)
@@ -623,19 +623,19 @@
     x_rows = alpha * start + step * direction
     r_rows = left - step * image
     for half in range(HALVES):
-        x_out[pl.ds(half * HALF, HALF)] = x_rows[half]
-        r_out[pl.ds(half * HALF, HALF)] = r_rows[half]
+        out[pl.ds(half * HALF, HALF)] = x_rows[half]
+        out[pl.ds((HALVES + half) * HALF, HALF)] = r_rows[half]
 
 
 def on_device(points, right_side, near_list, leaf_skeleton, top_index):
     vmem = pl.BlockSpec(memory_space=pltpu.VMEM)
     dma = pltpu.SemaphoreType.DMA
-    out = jax.ShapeDtypeStruct((HALVES * HALF,), F32)
-    solution_field, residual = pl.pallas_call(
+    out = jax.ShapeDtypeStruct((2 * HALVES * HALF,), F32)
+    both = pl.pallas_call(
         body,
-        out_shape=(out, out),
+        out_shape=out,
         in_specs=[pl.BlockSpec(memory_space=pl.ANY)] * 5,
-        out_specs=(vmem, vmem),
+        out_specs=vmem,
         scratch_shapes=[
             pltpu.VMEM((HALVES * HALF,), F32),
             pltpu.SMEM((LDEV, SLOTS), jnp.int32),
@@ -680,7 +680,7 @@
         ),
         name="ridge_cg",
     )(points, right_side, near_list, leaf_skeleton, top_index)
-    return solution_field, residual
+    return both[: HALVES * HALF], both[HALVES * HALF :]
 
 
 def solution(mesh):

time: 67.4 us -> 65.3 us (0.969)
  Pallas kernels: 64.6 us -> 63.1 us
    unnamed x4 -> x0, local copies, waits for them, and re-layouts: 1.92 us -> none
    pallas_call x1, Pallas kernels: 64.6 us -> 63.1 us  [on_device(): pl.pallas_call(body, out_shape=out, in_specs=[pl.BlockSpec(memory_space=p...]
    slice x0 -> x1, local copies, waits for them, and re-layouts: none -> 1.33 us  [on_device(): return (both[:HALVES * HALF], both[HALVES * HALF:])]
where the time goes in v6:
time: 65.3 us; the launch traced here: 65.1 us
  Pallas kernels  63.1 us (97%)
  local copies, waits for them, and re-layouts  1.33 us (2%)
    pallas_call x1, Pallas kernels, on_device(): pl.pallas_call(body, out_shape=out, in_specs=[pl.BlockSpec(memory_space=p...  63.1 us
    slice x1, local copies, waits for them, and re-layouts, on_device(): return (both[:HALVES * HALF], both[HALVES * HALF:])  1.33 us

profile of v6, /device:TPU:0, one launch (start us, length us, event | category | flops | bytes accessed | tf_op | source)
XLA Modules:
  0.0 65.1 jit_solution(7379622672785579521)
XLA Ops:
  0.6 63.1 %ridge_cg.1 = f32[6144]{0:T(1024)} custom-call(bf16[64,3072]{1,0:T(8,128)(2,1)} %pts_hbm.1, f32[3072]{0:T(1024)} %rhs_hbm.1, s32[3,6]{1,0:T(4,128)} %near_hbm.1, s32[3,256]{1,0:T(4,128)} %skel_hbm.1, s32[32]{0:T(128)} %top_hbm.1), custom_call_target="tpu_custom_call" | custom-call | tf_op jit(solution)/shard_map/ridge_cg/pallas_call | solution.py:634
  63.8 1.3 %fusion = (f32[3072]{0:T(1024)}, f32[3072]{0:T(1024)}) fusion(f32[6144]{0:T(1024)} %ridge_cg.1), kind=kLoop, calls=%fused_computation | loop fusion | bytes 49152 | tf_op jit(solution)/shard_map/slice | solution.py:683

commit v7 on v6

--- a/solution.py
+++ b/solution.py
@@ -191,8 +191,9 @@
                 pts_hbm.at[:, pl.ds(start, PARTS[wave])], pts[wave].at[MINE + half], in_s.at[4 + wave]
             ).start()
     for half in range(HALVES, 8):
-        vals[0, MINE + half] = jnp.zeros((1, HALF), F32)
-        vals[1, MINE + half] = jnp.zeros((1, HALF), F32)
+        for place in range(GAPS):
+            vals[0, 8 * place + half] = jnp.zeros((1, HALF), F32)
+            vals[1, 8 * place + half] = jnp.zeros((1, HALF), F32)
     for copy in loads:
         copy.wait()
     for wave in range(WAVES):
@@ -234,11 +235,11 @@
         for gap in remote_gaps:
             place = 8 * (gap + REACH)
             send(
-                vals.at[it, pl.ds(MINE, 8)], vals.at[it, pl.ds(place, 8)], va_s.at[it], va_r.at[it], tx=tx_at(-gap)
+                vals.at[it, pl.ds(MINE, HALVES)], vals.at[it, pl.ds(place, HALVES)], va_s.at[it], va_r.at[it], tx=tx_at(-gap)
             ).start()
 
     def values_here(it):
-        four = vals.at[it, pl.ds(0, 8 * (GAPS - 1))]
+        four = vals.at[it, pl.ds(0, HALVES * (GAPS - 1))]
         settle_both(four, (va_s.at[it], va_r.at[it]))
 
     def slot(leaf, number, half):
@@ -555,7 +556,7 @@
     slots(0, 1, 0, HALVES)
     points_here(2)
     remote_aux(2)
-    slots(0, 2, 0, HALVES)
+    slots(0, 2, 0, 3)
     settle_both(gt.at[pl.ds(0, N_TX - 1)], (g_s.at[1], g_r.at[1]))
     group_sources = row_sources(gt[...].reshape(N_TX * TSK, 128))
     kc[...] = jnp.exp2(
@@ -563,6 +564,7 @@
     )
     across(0)
     send_middle(0)
+    slots(0, 2, 3, HALVES)
     points_here(3)
     remote_aux(3)
     slots(0, 3, 0, HALVES)

time: 65.3 us -> 65.1 us (level)
  no operation moved by 1% of the time
where the time goes in v7:
time: 65.1 us; the launch traced here: 64.9 us
  Pallas kernels  62.9 us (97%)
  local copies, waits for them, and re-layouts  1.33 us (2%)
    pallas_call x1, Pallas kernels, on_device(): pl.pallas_call(body, out_shape=out, in_specs=[pl.BlockSpec(memory_space=p...  62.9 us
    slice x1, local copies, waits for them, and re-layouts, on_device(): return (both[:HALVES * HALF], both[HALVES * HALF:])  1.33 us

profile of v7, /device:TPU:0, one launch (start us, length us, event | category | flops | bytes accessed | tf_op | source)
XLA Modules:
  0.0 64.9 jit_solution(6381969546713816187)
XLA Ops:
  0.6 62.9 %ridge_cg.1 = f32[6144]{0:T(1024)} custom-call(bf16[64,3072]{1,0:T(8,128)(2,1)} %pts_hbm.1, f32[3072]{0:T(1024)} %rhs_hbm.1, s32[3,6]{1,0:T(4,128)} %near_hbm.1, s32[3,256]{1,0:T(4,128)} %skel_hbm.1, s32[32]{0:T(128)} %top_hbm.1), custom_call_target="tpu_custom_call" | custom-call | tf_op jit(solution)/shard_map/ridge_cg/pallas_call | solution.py:636
  63.5 1.3 %fusion = (f32[3072]{0:T(1024)}, f32[3072]{0:T(1024)}) fusion(f32[6144]{0:T(1024)} %ridge_cg.1), kind=kLoop, calls=%fused_computation | loop fusion | bytes 49152 | tf_op jit(solution)/shard_map/slice | solution.py:685
